TPU v7x, 512 devices: a whole 4x4x16 slice. The times are simulated.
512 devices in a mesh: ctx: 64 (over x, z), tp: 8 (over y, core).
Axes of the slice: x: 4, y: 4, z: 16, core: 2. Of those that a mesh axis runs over, the one named last changes fastest.
Arguments:
- queries: bfloat16 [8192, 4096], P(('ctx', 'tp')), may hold values from -8 to 8
- keys: bfloat16 [8192, 1024], P(('ctx', 'tp')), may hold values from -8 to 8
- values: bfloat16 [8192, 1024], P(('ctx', 'tp')), may hold values from -6 to 6
- out_grad: bfloat16 [8192, 4096], P(('ctx', 'tp')), may hold values from -6 to 6
- doc_lengths: int32 [8], replicated, may hold values from 1 to 2048, as said below
- doc_groups: int32 [8], replicated, may hold values from 0 to 1, as said below
Outputs:
- attn_out: bfloat16 [8192, 4096], P('ctx', 'tp')
- grad_q: bfloat16 [8192, 4096], P('ctx', 'tp')
- grad_k: bfloat16 [8192, 1024], P('ctx', 'tp')
- grad_v: bfloat16 [8192, 1024], P('ctx', 'tp')
Inputs may be any that keep to these rules, and one draw needn't show every extreme that they name: `doc_lengths`: the documents fill all 8192 tokens. The documents of one group (one value of doc_groups) have lengths that sum to 4096; each group holds 4 documents, exactly one of them of 2048 tokens. `doc_groups`: each group number is named by exactly 4 documents.
All inputs are finite; a program needn't handle non-finite values.
Results may differ from a plain program's by a relative error of at most 0.027.
Values may be sent and summed in bfloat16 or wider, within the bound.
A program may use at most 64 MiB of HBM per device.

v0:
```python
import math

import jax
import jax.numpy as jnp
from jax import lax
from jax.sharding import PartitionSpec as P

HD = 128
REP = 4


def partner(block, axis, apart):
    count = lax.axis_size(axis)
    route = []
    for low in range(count):
        high = low | 1 << apart
        if high != low and high < count:
            route += [(low, high), (high, low)]
    return lax.ppermute(block, axis, route)


def doc_tables(doc_lengths, doc_groups):
    doc_ends = jnp.cumsum(doc_lengths)
    starts = doc_ends - doc_lengths
    doc_order = jnp.arange(doc_lengths.shape[0], dtype=jnp.int32)
    same_group = (doc_groups[:, None] == doc_groups[None, :]) & (
        doc_order[None, :] < doc_order[:, None]
    )
    offsets = jnp.sum(jnp.where(same_group, doc_lengths[None, :], 0), axis=1)
    return (starts, doc_ends, offsets)


def slot_tokens(slot_ids, rows_dev, group_size, doc_lengths, doc_groups, starts, offsets):
    owner_id = slot_ids // rows_dev
    group_rank = slot_ids % rows_dev * group_size + owner_id % group_size
    group_id = owner_id // group_size
    matched = (doc_groups[None, :] == group_id[:, None]) & (offsets[None, :] <= group_rank[:, None])
    matched = matched & (group_rank[:, None] < (offsets + doc_lengths)[None, :])
    shift_base = jnp.sum(jnp.where(matched, (starts - offsets)[None, :], 0), axis=1)
    return shift_base + group_rank


def token_fields(tokens, group_size, doc_groups, starts, doc_ends, offsets):
    inside = (starts[None, :] <= tokens[:, None]) & (tokens[:, None] < doc_ends[None, :])
    doc_order = jnp.arange(starts.shape[0], dtype=jnp.int32)
    is_found = jnp.any(inside, axis=1)
    doc_ids = jnp.sum(jnp.where(inside, doc_order[None, :], 0), axis=1)
    doc_ids = jnp.where(is_found, doc_ids, -1)
    group_rank = jnp.sum(jnp.where(inside, (offsets - starts)[None, :], 0), axis=1) + tokens
    doc_group = jnp.sum(jnp.where(inside, doc_groups[None, :], 0), axis=1)
    owner_id = doc_group * group_size + group_rank % group_size
    return (doc_ids, owner_id)


def bucket_slots(owner_id, capacity):
    local_rows = jnp.arange(owner_id.shape[0], dtype=jnp.int32)
    earlier = (owner_id[None, :] == owner_id[:, None]) & (local_rows[None, :] < local_rows[:, None])
    return owner_id * capacity + jnp.sum(earlier, axis=1)


def arrival_slots(held_tokens, unit_rows, capacity):
    source = held_tokens // unit_rows
    local_rows = jnp.arange(held_tokens.shape[0], dtype=jnp.int32)
    earlier = (source[None, :] == source[:, None]) & (local_rows[None, :] < local_rows[:, None])
    return source * capacity + jnp.sum(earlier, axis=1)


def into_buckets(array, send_slot, capacity, owners):
    shaped = jnp.zeros((owners * capacity,) + array.shape[1:], array.dtype).at[send_slot].set(array)
    return shaped.reshape((owners, capacity) + array.shape[1:])


def attend(
    query_rows, grad_rows, query_tokens, query_docs, key_rows, value_rows, key_tokens, key_docs
):
    head_size = key_rows.shape[1]
    softmax_scale = head_size ** (-0.5)
    key_count = key_rows.shape[0]
    key_block = math.gcd(key_count, 128)
    blocks = key_count // key_block
    key_blocks = key_rows.reshape(blocks, key_block, head_size)
    value_blocks = value_rows.reshape(blocks, key_block, head_size)
    token_blocks = key_tokens.reshape(blocks, key_block)
    doc_blocks = key_docs.reshape(blocks, key_block)
    contract = (((1,), (1,)), ((), ()))
    across = (((0,), (0,)), ((), ()))
    query_count = query_rows.shape[0]

    def scored(key_piece, token_piece, doc_piece):
        scores = (
            lax.dot_general(query_rows, key_piece, contract, preferred_element_type=jnp.float32)
            * softmax_scale
        )
        allowed = (query_docs[:, None] == doc_piece[None, :]) & (
            token_piece[None, :] <= query_tokens[:, None]
        )
        return (scores, allowed)

    def running(running_state, block_data):
        highest, partial_mass = running_state
        scores, allowed = scored(*block_data)
        new_highest = jnp.maximum(highest, jnp.max(jnp.where(allowed, scores, -1e30), axis=1))
        fresh_mass = jnp.sum(
            jnp.where(allowed, jnp.exp(scores - new_highest[:, None]), 0.0), axis=1
        )
        partial_mass = partial_mass * jnp.exp(highest - new_highest) + fresh_mass
        return ((new_highest, partial_mass), None)

    initial = (jnp.full((query_count,), -1e30, jnp.float32), jnp.zeros((query_count,), jnp.float32))
    (highest, partial_mass), _ = lax.scan(running, initial, (key_blocks, token_blocks, doc_blocks))
    log_total = highest + jnp.log(partial_mass)

    def weighted(accumulated, block_data):
        key_piece, value_piece, token_piece, doc_piece = block_data
        scores, allowed = scored(key_piece, token_piece, doc_piece)
        weights = jnp.where(allowed, jnp.exp(scores - log_total[:, None]), 0.0).astype(jnp.bfloat16)
        return (
            accumulated + jnp.dot(weights, value_piece, preferred_element_type=jnp.float32),
            None,
        )

    blocks_data = (key_blocks, value_blocks, token_blocks, doc_blocks)
    accumulated, _ = lax.scan(
        weighted, jnp.zeros((query_count, head_size), jnp.float32), blocks_data
    )
    attention = accumulated.astype(jnp.bfloat16)
    delta = jnp.sum(grad_rows.astype(jnp.float32) * attention.astype(jnp.float32), axis=1)

    def gradients(query_sums, block_data):
        key_piece, value_piece, token_piece, doc_piece = block_data
        scores, allowed = scored(key_piece, token_piece, doc_piece)
        weights = jnp.where(allowed, jnp.exp(scores - log_total[:, None]), 0.0)
        value_terms = lax.dot_general(
            weights.astype(jnp.bfloat16), grad_rows, across, preferred_element_type=jnp.float32
        )
        grad_probs = lax.dot_general(
            grad_rows, value_piece, contract, preferred_element_type=jnp.float32
        )
        dscore = (weights * (grad_probs - delta[:, None])).astype(jnp.bfloat16)
        query_sums = query_sums + jnp.dot(dscore, key_piece, preferred_element_type=jnp.float32)
        key_terms = (
            lax.dot_general(dscore, query_rows, across, preferred_element_type=jnp.float32)
            * softmax_scale
        )
        return (query_sums, (key_terms, value_terms))

    query_sums, (key_terms, value_terms) = lax.scan(
        gradients, jnp.zeros((query_count, head_size), jnp.float32), blocks_data
    )
    query_grad = (query_sums * softmax_scale).astype(jnp.bfloat16)
    return (
        attention,
        query_grad,
        key_terms.reshape(key_count, head_size),
        value_terms.reshape(key_count, head_size),
    )


def body(queries, keys, values, out_grad, doc_lengths, doc_groups):
    sub_rows = queries.shape[0]
    tp_size = lax.axis_size("tp")
    owners = lax.axis_size("ctx")
    group_size = owners // 2
    bit_count = group_size.bit_length() - 1
    rows_dev = sub_rows * tp_size
    ctx_index = lax.axis_index("ctx")
    starts, doc_ends, offsets = doc_tables(doc_lengths, doc_groups)
    my_slots = ctx_index * rows_dev + jnp.arange(rows_dev, dtype=jnp.int32)
    held_tokens = slot_tokens(
        my_slots, rows_dev, group_size, doc_lengths, doc_groups, starts, offsets
    )
    held_docs, _ = token_fields(held_tokens, group_size, doc_groups, starts, doc_ends, offsets)
    head_queries = queries.reshape(sub_rows, tp_size, REP * HD)
    head_keys = keys.reshape(sub_rows, tp_size, HD)
    head_values = values.reshape(sub_rows, tp_size, HD)
    head_grads = out_grad.reshape(sub_rows, tp_size, REP * HD)
    by_heads = (
        lax.all_to_all(head_queries, "tp", split_axis=1, concat_axis=0, tiled=True),
        lax.all_to_all(head_keys, "tp", split_axis=1, concat_axis=0, tiled=True),
        lax.all_to_all(head_values, "tp", split_axis=1, concat_axis=0, tiled=True),
        lax.all_to_all(head_grads, "tp", split_axis=1, concat_axis=0, tiled=True),
    )
    seq_queries, seq_keys, seq_values, seq_grads = (
        moved_array.reshape(rows_dev, -1) for moved_array in by_heads
    )
    seq_tokens = ctx_index * rows_dev + jnp.arange(rows_dev, dtype=jnp.int32)
    seq_docs, destination = token_fields(
        seq_tokens, group_size, doc_groups, starts, doc_ends, offsets
    )
    capacity = (rows_dev + group_size - 1) // group_size
    send_slot = bucket_slots(destination, capacity)
    arrival = arrival_slots(held_tokens, rows_dev, capacity)
    arrived = (
        lax.all_to_all(
            into_buckets(seq_queries, send_slot, capacity, owners),
            "ctx",
            split_axis=0,
            concat_axis=0,
            tiled=True,
        ),
        lax.all_to_all(
            into_buckets(seq_keys, send_slot, capacity, owners),
            "ctx",
            split_axis=0,
            concat_axis=0,
            tiled=True,
        ),
        lax.all_to_all(
            into_buckets(seq_values, send_slot, capacity, owners),
            "ctx",
            split_axis=0,
            concat_axis=0,
            tiled=True,
        ),
        lax.all_to_all(
            into_buckets(seq_grads, send_slot, capacity, owners),
            "ctx",
            split_axis=0,
            concat_axis=0,
            tiled=True,
        ),
    )
    own_queries, own_keys, own_values, own_grads = (
        moved_array.reshape(owners * capacity, -1)[arrival] for moved_array in arrived
    )
    member = ctx_index % group_size
    group_key_rows, group_value_rows = (own_keys, own_values)
    for bit_level in range(bit_count):
        other_keys, other_values = partner((group_key_rows, group_value_rows), "ctx", bit_level)
        upper_half = member >> bit_level & 1 == 1
        group_key_rows = jnp.where(
            upper_half,
            jnp.concatenate([other_keys, group_key_rows]),
            jnp.concatenate([group_key_rows, other_keys]),
        )
        group_value_rows = jnp.where(
            upper_half,
            jnp.concatenate([other_values, group_value_rows]),
            jnp.concatenate([group_value_rows, other_values]),
        )
    group_slots = (ctx_index - member) * rows_dev + jnp.arange(
        group_size * rows_dev, dtype=jnp.int32
    )
    key_tokens = slot_tokens(
        group_slots, rows_dev, group_size, doc_lengths, doc_groups, starts, offsets
    )
    key_docs, _ = token_fields(key_tokens, group_size, doc_groups, starts, doc_ends, offsets)
    attention, query_grad, key_terms, value_terms = attend(
        own_queries.reshape(rows_dev * REP, HD),
        own_grads.reshape(rows_dev * REP, HD),
        jnp.repeat(held_tokens, REP),
        jnp.repeat(held_docs, REP),
        group_key_rows,
        group_value_rows,
        key_tokens,
        key_docs,
    )
    key_parts = key_terms.reshape(group_size, rows_dev, HD)
    value_parts = value_terms.reshape(group_size, rows_dev, HD)
    for bit_level in reversed(range(bit_count)):
        half_count = key_parts.shape[0] // 2
        upper_half = member >> bit_level & 1 == 1
        kept_keys = jnp.where(upper_half, key_parts[half_count:], key_parts[:half_count])
        kept_values = jnp.where(upper_half, value_parts[half_count:], value_parts[:half_count])
        sent_keys = jnp.where(upper_half, key_parts[:half_count], key_parts[half_count:])
        sent_values = jnp.where(upper_half, value_parts[:half_count], value_parts[half_count:])
        other_keys, other_values = partner((sent_keys, sent_values), "ctx", bit_level)
        key_parts = kept_keys + other_keys
        value_parts = kept_values + other_values
    attn_out = attention.reshape(rows_dev, REP * HD)
    grad_q = query_grad.reshape(rows_dev, REP * HD)
    grad_k = key_parts[0].astype(jnp.bfloat16)
    grad_v = value_parts[0].astype(jnp.bfloat16)
    return (attn_out, grad_q, grad_k, grad_v)


def solution(mesh):
    in_specs = (
        P(("ctx", "tp"), None),
        P(("ctx", "tp"), None),
        P(("ctx", "tp"), None),
        P(("ctx", "tp"), None),
        P(),
        P(),
    )
    out_specs = (P("ctx", "tp"), P("ctx", "tp"), P("ctx", "tp"), P("ctx", "tp"))
    return jax.shard_map(body, mesh=mesh, in_specs=in_specs, out_specs=out_specs, check_vma=False)
```

profile of v0, /device:TPU:34, one launch (start us, length us, event | category | flops | bytes accessed | tf_op | source)
XLA Modules:
  0.0 648.8 jit_solution(5469895167341269521)
XLA Ops:
  2.0 4.5 all-to-all-start
  11.9 4.7 all-to-all-start.4
  18.4 3.7 all-to-all-done.4
  27.1 4.4 all-to-all-done.2
  37.2 3.8 all-to-all-done.6
  41.0 18.2 %all-to-all-start.1 = ((bf16[64,4,128]{2,1,0:T(4,128)(2,1)}), bf16[64,4,128]{2,1,0:T(4,128)(2,1)S(1)}, u32[]{:S(2)}, u32[]{:S(2)}) async-start(bf16[64,4,128]{2,1,0:T(4,128)(2,1)} %bitcast.11), calls=%async_computation.1 | async-start | bytes 131072 | tf_op jit(solution)/shard_map/all_to_all | solution.py:201
  60.9 11.3 %all-to-all-done.1 = bf16[64,4,128]{2,1,0:T(4,128)(2,1)S(1)} async-done(((bf16[64,4,128]{2,1,0:T(4,128)(2,1)}), bf16[64,4,128]{2,1,0:T(4,128)(2,1)S(1)}, u32[]{:S(2)}, u32[]{:S(2)}) %all-to-all-start.1) | async-done | bytes 65568 | tf_op jit(solution)/shard_map/all_to_all | solution.py:201
  72.2 6.3 all-to-all-start.5
  83.6 7.9 %all-to-all-done.5 = bf16[64,4,128]{2,1,0:T(4,128)(2,1)S(1)} async-done(((bf16[64,4,128]{2,1,0:T(4,128)(2,1)}), bf16[64,4,128]{2,1,0:T(4,128)(2,1)S(1)}, u32[]{:S(2)}, u32[]{:S(2)}) %all-to-all-start.5) | async-done | bytes 65568 | tf_op jit(solution)/shard_map/all_to_all | solution.py:208
  91.5 7.3 %all-to-all-start.3 = ((bf16[64,4,512]{2,1,0:T(4,128)(2,1)}), bf16[64,4,512]{2,1,0:T(4,128)(2,1)S(1)}, u32[]{:S(2)}, u32[]{:S(2)}) async-start(bf16[64,4,512]{2,1,0:T(4,128)(2,1)} %reshape.575), calls=%async_computation.3 | async-start | bytes 524288 | tf_op jit(solution)/shard_map/all_to_all | solution.py:194
  102.1 4.3 collective-permute-start.1
  109.9 4.5 collective-permute-start.6
  114.4 6.9 %collective-permute-start.2 = (bf16[512,128]{1,0:T(8,128)(2,1)S(1)}, bf16[512,128]{1,0:T(8,128)(2,1)S(1)}, u32[]{:S(2)}, u32[]{:S(2)}) collective-permute-start(bf16[512,128]{1,0:T(8,128)(2,1)S(1)} %maximum_select_fusion.6), channel_id=1, source_target_pairs={{0,32},{32,0},{8,40},{40,8},{16,48},{48,16},{24,56},{56,24},{64,96... | collective-permute-start | bytes 393224 | tf_op jit(solution)/shard_map/ppermute | solution.py:19
  124.9 9.7 %collective-permute-done.2 = bf16[512,128]{1,0:T(8,128)(2,1)S(1)} collective-permute-done((bf16[512,128]{1,0:T(8,128)(2,1)S(1)}, bf16[512,128]{1,0:T(8,128)(2,1)S(1)}, u32[]{:S(2)}, u32[]{:S(2)}) %collective-permute-start.2) | collective-permute-done | bytes 131104 | tf_op jit(solution)/shard_map/ppermute | solution.py:19
  134.7 10.3 %collective-permute-start.3 = (bf16[1024,128]{1,0:T(8,128)(2,1)S(1)}, bf16[1024,128]{1,0:T(8,128)(2,1)S(1)}, u32[]{:S(2)}, u32[]{:S(2)}) collective-permute-start(bf16[1024,128]{1,0:T(8,128)(2,1)S(1)} %maximum_select_fusion.4), channel_id=1, source_target_pairs={{0,64},{64,0},{8,72},{72,8},{16,80},{80,16},{24,88},{88,24},{32,96... | collective-permute-start | bytes 786440 | tf_op jit(solution)/shard_map/ppermute | solution.py:19
  146.9 19.3 %all-to-all-start.7 = ((bf16[64,4,512]{2,1,0:T(4,128)(2,1)}), bf16[64,4,512]{2,1,0:T(4,128)(2,1)}, u32[]{:S(2)}, u32[]{:S(2)}) async-start(bf16[64,4,512]{2,1,0:T(4,128)(2,1)} %reshape.585), calls=%async_computation.7 | async-start | bytes 524288 | tf_op jit(solution)/shard_map/all_to_all | solution.py:215
  166.5 11.2 %collective-permute-start.8 = (bf16[1024,128]{1,0:T(8,128)(2,1)S(1)}, bf16[1024,128]{1,0:T(8,128)(2,1)}, u32[]{:S(2)}, u32[]{:S(2)}) collective-permute-start(bf16[1024,128]{1,0:T(8,128)(2,1)S(1)} %maximum_select_fusion.5), channel_id=1, source_target_pairs={{0,64},{64,0},{8,72},{72,8},{16,80},{80,16},{24,88},{88,24},{32,96... | collective-permute-start | bytes 786440 | tf_op jit(solution)/shard_map/ppermute | solution.py:19
  181.3 27.6 %collective-permute-done.8 = bf16[1024,128]{1,0:T(8,128)(2,1)} collective-permute-done((bf16[1024,128]{1,0:T(8,128)(2,1)S(1)}, bf16[1024,128]{1,0:T(8,128)(2,1)}, u32[]{:S(2)}, u32[]{:S(2)}) %collective-permute-start.8) | collective-permute-done | bytes 262176 | tf_op jit(solution)/shard_map/ppermute | solution.py:19
  220.0 50.4 %while.39 = (s32[]{:T(128)}, f32[512]{0:T(512)S(1)}, f32[512]{0:T(512)S(1)}, s32[32,128]{1,0:T(8,128)S(1)}, s32[32,128]{1,0:T(8,128)S(1)}, /*index=5*/bf16[32,12...) while((s32[]{:T(128)}, f32[512]{0:T(512)S(1)}, ...), condition=%wide.region_18.19_spmd.clone, body=%wide.region_15.18_spmd.clone.sunk | while | flops 17566208 | bytes 740488 | solution.py:110
  272.9 53.3 %while.40 = (s32[]{:T(128)}, f32[512,128]{1,0:T(8,128)S(1)}, s32[32,128]{1,0:T(8,128)S(1)}, s32[32,128]{1,0:T(8,128)S(1)}, bf16[32,128,128]{2,1,0:T(8,128)(2,1)}...) while((s32[]{:T(128)}, f32[512,128]{1,0:T(8,128)S(1)}, ...), condition=%wide.region_20.21_spmd.clone, body=%wide.region_19.20_spmd.clone.sunk | while | flops 34144256 | bytes 745098 | solution.py:123
  327.0 139.4 %while.41 = (s32[]{:T(128)}, f32[512,128]{1,0:T(8,128)S(1)}, f32[32,128,128]{2,1,0:T(8,128)}, f32[32,128,128]{2,1,0:T(8,128)S(1)}, s32[32,128]{1,0:T(8,128)S(1)}...) while((s32[]{:T(128)}, f32[512,128]{1,0:T(8,128)S(1)}, ...), condition=%wide.region_24.25_spmd.clone, body=%wide.region_23.24_spmd.clone.sunk | while | flops 84688896 | bytes 2482367 | solution.py:147
  474.9 22.0 %collective-permute-done.10 = f32[16,128,128]{2,1,0:T(8,128)S(1)} collective-permute-done((f32[16,128,128]{2,1,0:T(8,128)S(1)}, f32[16,128,128]{2,1,0:T(8,128)S(1)}, u32[]{:S(2)}, u32[]{:S(2)}) %collective-permute-start.10) | collective-permute-done | bytes 1048608 | tf_op jit(solution)/shard_map/ppermute | solution.py:19
  497.9 7.3 %collective-permute-start.11 = (f32[8,128,128]{2,1,0:T(8,128)}, f32[8,128,128]{2,1,0:T(8,128)S(1)}, u32[]{:S(2)}, u32[]{:S(2)}) collective-permute-start(f32[8,128,128]{2,1,0:T(8,128)} %slice_select_fusion.3), channel_id=1, source_target_pairs={{0,64},{64,0},{8,72},{72,8},{16,80},{80,16},{24,88},{88,24},{32,96... | collective-permute-start | bytes 1572872 | tf_op jit(solution)/shard_map/ppermute | solution.py:19
  505.2 12.5 %collective-permute-done.15 = f32[16,128,128]{2,1,0:T(8,128)S(1)} collective-permute-done((f32[16,128,128]{2,1,0:T(8,128)S(1)}, f32[16,128,128]{2,1,0:T(8,128)S(1)}, u32[]{:S(2)}, u32[]{:S(2)}) %collective-permute-start.15) | collective-permute-done | bytes 1048608 | tf_op jit(solution)/shard_map/ppermute | solution.py:19
  518.7 7.7 %collective-permute-start.16 = (f32[8,128,128]{2,1,0:T(8,128)}, f32[8,128,128]{2,1,0:T(8,128)S(1)}, u32[]{:S(2)}, u32[]{:S(2)}) collective-permute-start(f32[8,128,128]{2,1,0:T(8,128)} %slice_select_fusion.2), channel_id=1, source_target_pairs={{0,64},{64,0},{8,72},{72,8},{16,80},{80,16},{24,88},{88,24},{32,96... | collective-permute-start | bytes 1572872 | tf_op jit(solution)/shard_map/ppermute | solution.py:19
  530.4 34.7 %collective-permute-done.11 = f32[8,128,128]{2,1,0:T(8,128)S(1)} collective-permute-done((f32[8,128,128]{2,1,0:T(8,128)}, f32[8,128,128]{2,1,0:T(8,128)S(1)}, u32[]{:S(2)}, u32[]{:S(2)}) %collective-permute-start.11) | collective-permute-done | bytes 524320 | tf_op jit(solution)/shard_map/ppermute | solution.py:19
  567.1 9.7 %collective-permute-done.16 = f32[8,128,128]{2,1,0:T(8,128)S(1)} collective-permute-done((f32[8,128,128]{2,1,0:T(8,128)}, f32[8,128,128]{2,1,0:T(8,128)S(1)}, u32[]{:S(2)}, u32[]{:S(2)}) %collective-permute-start.16) | collective-permute-done | bytes 524320 | tf_op jit(solution)/shard_map/ppermute | solution.py:19
  578.9 26.0 %collective-permute-done.12 = f32[4,128,128]{2,1,0:T(8,128)S(1)} collective-permute-done((f32[4,128,128]{2,1,0:T(8,128)S(1)}, f32[4,128,128]{2,1,0:T(8,128)S(1)}, u32[]{:S(2)}, u32[]{:S(2)}) %collective-permute-start.12) | collective-permute-done | bytes 262176 | tf_op jit(solution)/shard_map/ppermute | solution.py:19
  604.9 17.5 %collective-permute-start.13 = (f32[2,128,128]{2,1,0:T(8,128)S(1)}, f32[2,128,128]{2,1,0:T(8,128)S(1)}, u32[]{:S(2)}, u32[]{:S(2)}) collective-permute-start(f32[2,128,128]{2,1,0:T(8,128)S(1)} %slice_select_fusion.7), channel_id=1, source_target_pairs={{0,16},{16,0},{8,24},{24,8},{32,48},{48,32},{40,56},{56,40},{64,80... | collective-permute-start | bytes 393224 | tf_op jit(solution)/shard_map/ppermute | solution.py:19
  622.6 5.4 collective-permute-start.18
  628.0 4.9 collective-permute-done.13
  633.0 8.9 %collective-permute-start.14 = (f32[1,128,128]{2,1,0:T(8,128)S(1)}, f32[1,128,128]{2,1,0:T(8,128)S(1)}, u32[]{:S(2)}, u32[]{:S(2)}) collective-permute-start(f32[1,128,128]{2,1,0:T(8,128)S(1)} %slice_select_fusion.9), channel_id=1, source_target_pairs={{0,8},{8,0},{16,24},{24,16},{32,40},{40,32},{48,56},{56,48},{64,72... | collective-permute-start | bytes 196616 | tf_op jit(solution)/shard_map/ppermute | solution.py:19
  (952 shorter events, 321.1 us)
Async XLA Ops:
  2.0 9.9 %all-to-all-start = ((bf16[16,8,128]{2,0,1:T(8,128)(2,1)}), bf16[16,8,128]{2,0,1:T(8,128)(2,1)S(1)}, u32[]{:S(2)}, u32[]{:S(2)}) async-start(bf16[16,8,128]{2,0,1:T(8,128)(2,1)} %copy_bitcast_fusion.3), calls=%async_computation | async-start | bytes 65536 | tf_op jit(solution)/shard_map/all_to_all | solution.py:179
  11.9 10.2 %all-to-all-start.4 = ((bf16[16,8,128]{2,0,1:T(8,128)(2,1)}), bf16[16,8,128]{2,0,1:T(8,128)(2,1)S(1)}, u32[]{:S(2)}, u32[]{:S(2)}) async-start(bf16[16,8,128]{2,0,1:T(8,128)(2,1)} %copy_bitcast_fusion.2), calls=%async_computation.4 | async-start | bytes 65536 | tf_op jit(solution)/shard_map/all_to_all | solution.py:180
  22.1 9.4 %all-to-all-start.2 = ((bf16[16,8,512]{2,0,1:T(8,128)(2,1)}), bf16[16,8,512]{2,0,1:T(8,128)(2,1)S(1)}, u32[]{:S(2)}, u32[]{:S(2)}) async-start(bf16[16,8,512]{2,0,1:T(8,128)(2,1)} %bitcast.149), calls=%async_computation.2 | async-start | bytes 262144 | tf_op jit(solution)/shard_map/all_to_all | solution.py:178
  31.5 9.4 %all-to-all-start.6 = ((bf16[16,8,512]{2,0,1:T(8,128)(2,1)}), bf16[16,8,512]{2,0,1:T(8,128)(2,1)S(1)}, u32[]{:S(2)}, u32[]{:S(2)}) async-start(bf16[16,8,512]{2,0,1:T(8,128)(2,1)} %bitcast.148), calls=%async_computation.6 | async-start | bytes 262144 | tf_op jit(solution)/shard_map/all_to_all | solution.py:181
  41.0 31.2 %all-to-all-start.1 = ((bf16[64,4,128]{2,1,0:T(4,128)(2,1)}), bf16[64,4,128]{2,1,0:T(4,128)(2,1)S(1)}, u32[]{:S(2)}, u32[]{:S(2)}) async-start(bf16[64,4,128]{2,1,0:T(4,128)(2,1)} %bitcast.11), calls=%async_computation.1 | async-start | bytes 131072 | tf_op jit(solution)/shard_map/all_to_all | solution.py:201
  72.2 19.3 %all-to-all-start.5 = ((bf16[64,4,128]{2,1,0:T(4,128)(2,1)}), bf16[64,4,128]{2,1,0:T(4,128)(2,1)S(1)}, u32[]{:S(2)}, u32[]{:S(2)}) async-start(bf16[64,4,128]{2,1,0:T(4,128)(2,1)} %bitcast.23), calls=%async_computation.5 | async-start | bytes 131072 | tf_op jit(solution)/shard_map/all_to_all | solution.py:208
  81.1 20.9 %collective-permute-start = (bf16[128,128]{1,0:T(8,128)(2,1)S(1)}, bf16[128,128]{1,0:T(8,128)(2,1)S(1)}, u32[]{:S(2)}, u32[]{:S(2)}) collective-permute-start(bf16[128,128]{1,0:T(8,128)(2,1)S(1)} %gather_fusion), channel_id=1, source_target_pairs={{0,8},{8,0},{16,24},{24,16},{32,40},{40,32},{48,56},{56,48},{64,72... | collective-permute-start | bytes 98312 | tf_op jit(solution)/shard_map/ppermute | solution.py:19
  91.5 55.4 %all-to-all-start.3 = ((bf16[64,4,512]{2,1,0:T(4,128)(2,1)}), bf16[64,4,512]{2,1,0:T(4,128)(2,1)S(1)}, u32[]{:S(2)}, u32[]{:S(2)}) async-start(bf16[64,4,512]{2,1,0:T(4,128)(2,1)} %reshape.575), calls=%async_computation.3 | async-start | bytes 524288 | tf_op jit(solution)/shard_map/all_to_all | solution.py:194
  99.5 10.3 %collective-permute-start.5 = (bf16[128,128]{1,0:T(8,128)(2,1)S(1)}, bf16[128,128]{1,0:T(8,128)(2,1)S(1)}, u32[]{:S(2)}, u32[]{:S(2)}) collective-permute-start(bf16[128,128]{1,0:T(8,128)(2,1)S(1)} %gather_fusion.2), channel_id=1, source_target_pairs={{0,8},{8,0},{16,24},{24,16},{32,40},{40,32},{48,56},{56,48},{64,72... | collective-permute-start | bytes 98312 | tf_op jit(solution)/shard_map/ppermute | solution.py:19
  102.1 12.3 %collective-permute-start.1 = (bf16[256,128]{1,0:T(8,128)(2,1)S(1)}, bf16[256,128]{1,0:T(8,128)(2,1)S(1)}, u32[]{:S(2)}, u32[]{:S(2)}) collective-permute-start(bf16[256,128]{1,0:T(8,128)(2,1)S(1)} %maximum_select_fusion.8), channel_id=1, source_target_pairs={{0,16},{16,0},{8,24},{24,8},{32,48},{48,32},{40,56},{56,40},{64,80... | collective-permute-start | bytes 196616 | tf_op jit(solution)/shard_map/ppermute | solution.py:19
  109.9 11.5 %collective-permute-start.6 = (bf16[256,128]{1,0:T(8,128)(2,1)S(1)}, bf16[256,128]{1,0:T(8,128)(2,1)S(1)}, u32[]{:S(2)}, u32[]{:S(2)}) collective-permute-start(bf16[256,128]{1,0:T(8,128)(2,1)S(1)} %maximum_select_fusion.9), channel_id=1, source_target_pairs={{0,16},{16,0},{8,24},{24,8},{32,48},{48,32},{40,56},{56,40},{64,80... | collective-permute-start | bytes 196616 | tf_op jit(solution)/shard_map/ppermute | solution.py:19
  114.4 20.2 %collective-permute-start.2 = (bf16[512,128]{1,0:T(8,128)(2,1)S(1)}, bf16[512,128]{1,0:T(8,128)(2,1)S(1)}, u32[]{:S(2)}, u32[]{:S(2)}) collective-permute-start(bf16[512,128]{1,0:T(8,128)(2,1)S(1)} %maximum_select_fusion.6), channel_id=1, source_target_pairs={{0,32},{32,0},{8,40},{40,8},{16,48},{48,16},{24,56},{56,24},{64,96... | collective-permute-start | bytes 393224 | tf_op jit(solution)/shard_map/ppermute | solution.py:19
  121.4 45.0 %collective-permute-start.7 = (bf16[512,128]{1,0:T(8,128)(2,1)S(1)}, bf16[512,128]{1,0:T(8,128)(2,1)S(1)}, u32[]{:S(2)}, u32[]{:S(2)}) collective-permute-start(bf16[512,128]{1,0:T(8,128)(2,1)S(1)} %maximum_select_fusion.7), channel_id=1, source_target_pairs={{0,32},{32,0},{8,40},{40,8},{16,48},{48,16},{24,56},{56,24},{64,96... | collective-permute-start | bytes 393224 | tf_op jit(solution)/shard_map/ppermute | solution.py:19
  134.7 43.1 %collective-permute-start.3 = (bf16[1024,128]{1,0:T(8,128)(2,1)S(1)}, bf16[1024,128]{1,0:T(8,128)(2,1)S(1)}, u32[]{:S(2)}, u32[]{:S(2)}) collective-permute-start(bf16[1024,128]{1,0:T(8,128)(2,1)S(1)} %maximum_select_fusion.4), channel_id=1, source_target_pairs={{0,64},{64,0},{8,72},{72,8},{16,80},{80,16},{24,88},{88,24},{32,96... | collective-permute-start | bytes 786440 | tf_op jit(solution)/shard_map/ppermute | solution.py:19
  146.9 66.8 %all-to-all-start.7 = ((bf16[64,4,512]{2,1,0:T(4,128)(2,1)}), bf16[64,4,512]{2,1,0:T(4,128)(2,1)}, u32[]{:S(2)}, u32[]{:S(2)}) async-start(bf16[64,4,512]{2,1,0:T(4,128)(2,1)} %reshape.585), calls=%async_computation.7 | async-start | bytes 524288 | tf_op jit(solution)/shard_map/all_to_all | solution.py:215
  166.5 42.4 %collective-permute-start.8 = (bf16[1024,128]{1,0:T(8,128)(2,1)S(1)}, bf16[1024,128]{1,0:T(8,128)(2,1)}, u32[]{:S(2)}, u32[]{:S(2)}) collective-permute-start(bf16[1024,128]{1,0:T(8,128)(2,1)S(1)} %maximum_select_fusion.5), channel_id=1, source_target_pairs={{0,64},{64,0},{8,72},{72,8},{16,80},{80,16},{24,88},{88,24},{32,96... | collective-permute-start | bytes 786440 | tf_op jit(solution)/shard_map/ppermute | solution.py:19
  178.7 38.5 %collective-permute-start.4 = (bf16[2048,128]{1,0:T(8,128)(2,1)}, bf16[2048,128]{1,0:T(8,128)(2,1)}, u32[]{:S(2)}, u32[]{:S(2)}) collective-permute-start(bf16[2048,128]{1,0:T(8,128)(2,1)} %maximum_select_fusion.2), channel_id=1, source_target_pairs={{0,128},{128,0},{8,136},{136,8},{16,144},{144,16},{24,152},{152,24... | collective-permute-start | bytes 1572872 | tf_op jit(solution)/shard_map/ppermute | solution.py:19
  210.1 60.4 %collective-permute-start.9 = (bf16[2048,128]{1,0:T(8,128)(2,1)S(1)}, bf16[2048,128]{1,0:T(8,128)(2,1)}, u32[]{:S(2)}, u32[]{:S(2)}) collective-permute-start(bf16[2048,128]{1,0:T(8,128)(2,1)S(1)} %maximum_select_fusion.3), channel_id=1, source_target_pairs={{0,128},{128,0},{8,136},{136,8},{16,144},{144,16},{24,152},{152,24... | collective-permute-start | bytes 1572872 | tf_op jit(solution)/shard_map/ppermute | solution.py:19
  270.4 2.5 copy-start.4
  466.3 6.1 copy-start.1
  468.7 28.1 %copy-start.3 = (f32[32,128,128]{2,1,0:T(8,128)S(1)}, f32[32,128,128]{2,1,0:T(8,128)}, u32[]{:S(2)}) copy-start(f32[32,128,128]{2,1,0:T(8,128)} %get-tuple-element.182) | copy-start | bytes 6291460
  468.8 28.1 %collective-permute-start.10 = (f32[16,128,128]{2,1,0:T(8,128)S(1)}, f32[16,128,128]{2,1,0:T(8,128)S(1)}, u32[]{:S(2)}, u32[]{:S(2)}) collective-permute-start(f32[16,128,128]{2,1,0:T(8,128)S(1)} %slice_select_fusion.1), channel_id=1, source_target_pairs={{0,128},{128,0},{8,136},{136,8},{16,144},{144,16},{24,152},{152,24... | collective-permute-start | bytes 3145736 | tf_op jit(solution)/shard_map/ppermute | solution.py:19
  472.4 45.2 %collective-permute-start.15 = (f32[16,128,128]{2,1,0:T(8,128)S(1)}, f32[16,128,128]{2,1,0:T(8,128)S(1)}, u32[]{:S(2)}, u32[]{:S(2)}) collective-permute-start(f32[16,128,128]{2,1,0:T(8,128)S(1)} %slice_select_fusion), channel_id=1, source_target_pairs={{0,128},{128,0},{8,136},{136,8},{16,144},{144,16},{24,152},{152,24... | collective-permute-start | bytes 3145736 | tf_op jit(solution)/shard_map/ppermute | solution.py:19
  474.9 42.8 %copy-start.2 = (f32[32,128,128]{2,1,0:T(8,128)S(1)}, f32[32,128,128]{2,1,0:T(8,128)}, u32[]{:S(2)}) copy-start(f32[32,128,128]{2,1,0:T(8,128)} %copy-done.1) | copy-start | bytes 6291460
  497.9 67.2 %collective-permute-start.11 = (f32[8,128,128]{2,1,0:T(8,128)}, f32[8,128,128]{2,1,0:T(8,128)S(1)}, u32[]{:S(2)}, u32[]{:S(2)}) collective-permute-start(f32[8,128,128]{2,1,0:T(8,128)} %slice_select_fusion.3), channel_id=1, source_target_pairs={{0,64},{64,0},{8,72},{72,8},{16,80},{80,16},{24,88},{88,24},{32,96... | collective-permute-start | bytes 1572872 | tf_op jit(solution)/shard_map/ppermute | solution.py:19
  518.7 58.1 %collective-permute-start.16 = (f32[8,128,128]{2,1,0:T(8,128)}, f32[8,128,128]{2,1,0:T(8,128)S(1)}, u32[]{:S(2)}, u32[]{:S(2)}) collective-permute-start(f32[8,128,128]{2,1,0:T(8,128)} %slice_select_fusion.2), channel_id=1, source_target_pairs={{0,64},{64,0},{8,72},{72,8},{16,80},{80,16},{24,88},{88,24},{32,96... | collective-permute-start | bytes 1572872 | tf_op jit(solution)/shard_map/ppermute | solution.py:19
  565.2 39.7 %collective-permute-start.12 = (f32[4,128,128]{2,1,0:T(8,128)S(1)}, f32[4,128,128]{2,1,0:T(8,128)S(1)}, u32[]{:S(2)}, u32[]{:S(2)}) collective-permute-start(f32[4,128,128]{2,1,0:T(8,128)S(1)} %slice_select_fusion.5), channel_id=1, source_target_pairs={{0,32},{32,0},{8,40},{40,8},{16,48},{48,16},{24,56},{56,24},{64,96... | collective-permute-start | bytes 786440 | tf_op jit(solution)/shard_map/ppermute | solution.py:19
  577.0 45.5 %collective-permute-start.17 = (f32[4,128,128]{2,1,0:T(8,128)S(1)}, f32[4,128,128]{2,1,0:T(8,128)S(1)}, u32[]{:S(2)}, u32[]{:S(2)}) collective-permute-start(f32[4,128,128]{2,1,0:T(8,128)S(1)} %slice_select_fusion.4), channel_id=1, source_target_pairs={{0,32},{32,0},{8,40},{40,8},{16,48},{48,16},{24,56},{56,24},{64,96... | collective-permute-start | bytes 786440 | tf_op jit(solution)/shard_map/ppermute | solution.py:19
  604.9 28.0 %collective-permute-start.13 = (f32[2,128,128]{2,1,0:T(8,128)S(1)}, f32[2,128,128]{2,1,0:T(8,128)S(1)}, u32[]{:S(2)}, u32[]{:S(2)}) collective-permute-start(f32[2,128,128]{2,1,0:T(8,128)S(1)} %slice_select_fusion.7), channel_id=1, source_target_pairs={{0,16},{16,0},{8,24},{24,8},{32,48},{48,32},{40,56},{56,40},{64,80... | collective-permute-start | bytes 393224 | tf_op jit(solution)/shard_map/ppermute | solution.py:19
  622.6 19.3 %collective-permute-start.18 = (f32[2,128,128]{2,1,0:T(8,128)S(1)}, f32[2,128,128]{2,1,0:T(8,128)S(1)}, u32[]{:S(2)}, u32[]{:S(2)}) collective-permute-start(f32[2,128,128]{2,1,0:T(8,128)S(1)} %slice_select_fusion.6), channel_id=1, source_target_pairs={{0,16},{16,0},{8,24},{24,8},{32,48},{48,32},{40,56},{56,40},{64,80... | collective-permute-start | bytes 393224 | tf_op jit(solution)/shard_map/ppermute | solution.py:19
  633.0 11.6 %collective-permute-start.14 = (f32[1,128,128]{2,1,0:T(8,128)S(1)}, f32[1,128,128]{2,1,0:T(8,128)S(1)}, u32[]{:S(2)}, u32[]{:S(2)}) collective-permute-start(f32[1,128,128]{2,1,0:T(8,128)S(1)} %slice_select_fusion.9), channel_id=1, source_target_pairs={{0,8},{8,0},{16,24},{24,16},{32,40},{40,32},{48,56},{56,48},{64,72... | collective-permute-start | bytes 196616 | tf_op jit(solution)/shard_map/ppermute | solution.py:19
  642.0 6.2 collective-permute-start.19
  (1 other events, 0.8 us)
where the time goes:
time: 662 us; the launch traced here: 649 us
  matrix products  197 us (30%)
  waiting for transfers between devices  185 us (28%)
  starting transfers between devices  177 us (27%)
  local copies, waits for them, and re-layouts  59.5 us (9%)
  other arithmetic  25.7 us (4%)
    ppermute x20, waiting for transfers between devices, partner(): return lax.ppermute(block, axis, route)  153 us
    ppermute x20, starting transfers between devices, partner(): return lax.ppermute(block, axis, route)  110 us
    dot_general x64, matrix products, scored(): lax.dot_general(query_rows, key_piece, contract, preferred_element_type=j...  63 us
    dot_general x32, matrix products, weighted(): jnp.dot(weights, value_piece, preferred_element_type=jnp.float32)  39.6 us
    dot_general x32, matrix products, gradients(): jnp.dot(dscore, key_piece, preferred_element_type=jnp.float32)  32.2 us
    dot_general x32, matrix products, gradients(): lax.dot_general(grad_rows, value_piece, contract, preferred_element_type=...  30.5 us
    dot_general x32, matrix products, gradients(): lax.dot_general(dscore, query_rows, across, preferred_element_type=jnp.fl...  25.9 us
    all_to_all x1, starting transfers between devices, body(): lax.all_to_all(into_buckets(seq_grads, send_slot, capacity, owners), 'ctx...  19.3 us
  transfers between devices with their start and end apart: 28, of which 16 were waited for; matrix products, arithmetic and copies ran while one was open for 13% of the time, Pallas kernels for 0%

commit v1 on v0

v1 whole, which is shorter than its diff:
```python
import jax
import jax.numpy as jnp
from jax import lax
from jax.experimental import pallas as pl
from jax.experimental.pallas import tpu as pltpu
from jax.sharding import PartitionSpec as P

HD = 128
REP = 4
BLK = 128
XN = 4
ZN = 16
CTX = XN * ZN
TP = 8
NDOC = 8
HOPS = 8
SCALE = HD ** (-0.5)
SCALE2 = SCALE * 1.4426950408889634
NEG = -1e30
ZR = 48
ZK = 32
MESH = pl.DeviceIdType.MESH
NT = (((1,), (1,)), ((), ()))
NN = (((1,), (0,)), ((), ()))
TN = (((0,), (0,)), ((), ()))
F32 = jnp.float32
BF16 = jnp.bfloat16


def mm(a, b, dims):
    return lax.dot_general(a, b, dims, preferred_element_type=F32)


def lane_iota(width):
    return lax.broadcasted_iota(jnp.int32, (1, width), 1)


def kernel(
    len_ref, grp_ref, q_in, k_in, v_in, g_in,
    o_out, dq_out, dk_out, dv_out,
    qin, gin, kbuf, vbuf, qs, gs, ot, obf, m_ref, l_ref, d_ref, dqt, dqbf, low_ref,
    rs_send, rs_recv, zsend, zrecv, zsend_k, zrecv_k, xsend, xrecv, xsend_k, xrecv_k,
    az, ax, azk, axk, bfin, code_z, code_x, code_zk, code_xk,
    a_ss, a_rs, ag_ss, ag_rs, rs_ss, rs_rs, z_ss, z_rs, x_ss, x_rs, loc_s,
):
    c = lax.axis_index("ctx")
    me = lax.axis_index("tp")
    xi = c // ZN
    zi = c % ZN
    nxt = (c + 1) % CTX
    prv = (c + CTX - 1) % CTX
    up = (c + ZN) % CTX
    down = (c + CTX - ZN) % CTX

    barrier = pltpu.get_barrier_semaphore()

    def greet(ci, pi):
        pl.semaphore_signal(barrier, inc=1, device_id=(ci, pi), device_id_type=MESH)

    @pl.loop(1, TP)
    def _(i):
        greet(c, (me + i) % TP)

    @pl.loop(1, ZN)
    def _(i):
        greet(xi * ZN + (zi + i) % ZN, me)

    @pl.loop(1, XN)
    def _(i):
        greet((xi + i) % XN * ZN + zi, me)

    greet(nxt, me)
    greet(prv, me)
    pl.semaphore_wait(barrier, TP - 1 + ZN - 1 + XN - 1 + 2)

    kinds = (
        (k_in, kbuf.at[0], HD),
        (v_in, vbuf.at[0], HD),
        (q_in, qin, REP * HD),
        (g_in, gin, REP * HD),
    )

    def sent_piece(kind, peer):
        src, dst, width = kinds[kind]
        return pltpu.make_async_remote_copy(
            src_ref=src.at[:, pl.ds(pl.multiple_of(peer * width, width), width)],
            dst_ref=dst.at[pl.ds(pl.multiple_of(me * 16, 16), 16), :],
            send_sem=a_ss.at[kind, peer],
            recv_sem=a_rs.at[kind, me],
            device_id=(c, peer),
            device_id_type=MESH,
        )

    def got_piece(kind, peer):
        src, dst, width = kinds[kind]
        return pltpu.make_async_remote_copy(
            src_ref=src.at[:, pl.ds(pl.multiple_of(peer * width, width), width)],
            dst_ref=dst.at[pl.ds(pl.multiple_of(peer * 16, 16), 16), :],
            send_sem=a_ss.at[kind, peer],
            recv_sem=a_rs.at[kind, peer],
            device_id=(c, peer),
            device_id_type=MESH,
        )

    def own_piece(kind):
        src, dst, width = kinds[kind]
        return pltpu.make_async_copy(
            src.at[:, pl.ds(pl.multiple_of(me * width, width), width)],
            dst.at[pl.ds(pl.multiple_of(me * 16, 16), 16), :],
            loc_s.at[kind],
        )

    for kind in range(4):

        @pl.loop(1, TP)
        def _(i, kind=kind):
            sent_piece(kind, (me + i) % TP).start()

        own_piece(kind).start()

    lens = [len_ref[d] for d in range(NDOC)]
    first = [1 - grp_ref[d] for d in range(NDOC)]
    starts = []
    total = jnp.int32(0)
    for d in range(NDOC):
        starts.append(total)
        total = total + lens[d]

    def count0(position):
        acc = 0
        for d in range(NDOC):
            acc = acc + first[d] * jnp.minimum(jnp.maximum(position - starts[d], 0), lens[d])
        return acc

    base = c * BLK
    jl = lane_iota(REP * BLK)
    tok = base + (jl & (BLK - 1))
    low = jnp.zeros_like(tok)
    for d in range(NDOC):
        low = jnp.maximum(low, jnp.where(tok >= starts[d], starts[d], 0))
    low_ref[...] = low - base

    r0 = count0(base)
    c0 = (count0(base + BLK) - r0 + 15) >> 4
    r1 = base - r0
    before = count0(tok)
    is0 = count0(tok + 1) - before == 1
    rank = jnp.where(is0, before, tok - before)
    k = jnp.where(is0, (rank - r0) >> 4, c0 + ((rank - r1) >> 4))
    zd = rank & (ZN - 1)
    code_z[...] = zd * ZR + k * REP + (jl >> 7)
    half = slice(0, 2 * BLK)
    code_zk[...] = zd[:, half] * ZK + k[:, half] + 9 * (jl[:, half] >> 7)

    row0 = count0(xi * (ZN * BLK))
    row1 = xi * (ZN * BLK) - row0

    def arrived(zs, k):
        begin = (xi * ZN + zs) * BLK
        r0 = count0(begin)
        r0e = count0(begin + BLK)
        r1 = begin - r0
        r1e = begin + BLK - r0e
        c0 = (r0e - r0 + 15) >> 4
        g0 = k < c0
        kk = jnp.where(g0, k, k - c0)
        rb = jnp.where(g0, r0, r1)
        re = jnp.where(g0, r0e, r1e)
        rank = rb + ((zi - rb) & (ZN - 1)) + ZN * kk
        xd = jnp.where(g0, 0, 2) + ((rank >> 4) & 1)
        q = (rank - jnp.where(g0, row0, row1)) >> 5
        return rank < re, xd, q

    jx = lane_iota(ZN * ZR)
    zs = (jx * 43691) >> 21
    rem = jx - ZR * zs
    ok, xd, q = arrived(zs, rem >> 2)
    code_x[...] = jnp.where(ok, xd * 256 + (rem & 3) * 64 + q, -1)
    jk = lane_iota(ZN * ZK)
    e = jk & (ZK - 1)
    kv = jnp.where(e >= 9, 1, 0)
    ok, xd, q = arrived(jk >> 5, e - 9 * kv)
    code_xk[...] = jnp.where(ok, xd * 128 + kv * 64 + q, -1)

    jf = lane_iota(4 * 64)
    xs = jf >> 6
    g1 = xi // 2
    res = (xi % 2) * ZN + zi
    rs0 = count0(xs * (ZN * BLK))
    rs0e = count0((xs + 1) * (ZN * BLK))
    rsb = jnp.where(g1 == 1, xs * (ZN * BLK) - rs0, rs0)
    rse = jnp.where(g1 == 1, (xs + 1) * (ZN * BLK) - rs0e, rs0e)
    rank = rsb + ((res - rsb) & 31) + 32 * (jf & 63)
    code = jnp.where(rank < rse, rank >> 5, -1)
    bfin[...] = jnp.where(
        lax.broadcasted_iota(jnp.int32, (BLK, 256), 0) == code, 1.0, 0.0
    ).astype(BF16)

    def onehot(dst, code, rows, step):
        begin = pl.multiple_of(step * rows, rows)
        ids = begin + lax.broadcasted_iota(jnp.int32, (rows, dst.shape[1]), 0)
        dst[pl.ds(begin, rows), :] = jnp.where(ids == code[...], 1.0, 0.0).astype(BF16)

    def chain(buf, which, src_pos, dst_pos, to):
        return pltpu.make_async_remote_copy(
            src_ref=buf.at[src_pos],
            dst_ref=buf.at[dst_pos],
            send_sem=ag_ss.at[dst_pos, which],
            recv_sem=ag_rs.at[dst_pos, which],
            device_id=(to, me),
            device_id_type=MESH,
        )

    def take(kind):
        @pl.loop(1, TP)
        def _(i):
            got_piece(kind, (me + i) % TP).wait_recv()

        own_piece(kind).wait()

    for which, buf in ((0, kbuf), (1, vbuf)):
        take(which)
        chain(buf, which, 0, 1, nxt).start()
        chain(buf, which, 0, 2, up).start()

    take(2)
    for h in range(REP):
        qs[h * BLK : (h + 1) * BLK, :] = qin[:, h * HD : (h + 1) * HD]

    heads = [slice(h * BLK, (h + 1) * BLK) for h in range(REP)]
    key_row = lax.broadcasted_iota(jnp.int32, (BLK, BLK), 0)
    query_col = lax.broadcasted_iota(jnp.int32, (BLK, BLK), 1)

    def diag_scores(hs):
        raw = mm(kbuf[0], qs[hs, :], NT) * SCALE2
        return jnp.where((key_row <= query_col) & (key_row >= low_ref[:, hs]), raw, NEG)

    for hs in heads:
        s2 = diag_scores(hs)
        m = jnp.max(s2, axis=0, keepdims=True)
        p = jnp.exp2(s2 - m)
        m_ref[:, hs] = m
        l_ref[:, hs] = jnp.sum(p, axis=0, keepdims=True)
        ot[:, hs] = mm(vbuf[0], p.astype(BF16), TN)

    def pair_shift(s):
        rows = lax.broadcasted_iota(jnp.int32, (2 * BLK, BLK), 0)
        return jnp.where(rows < BLK, rows - BLK * s, rows - BLK - BLK * (2 * HOPS + 1 - s))

    def pair(buf, s):
        return buf[pl.ds(2 * s - 1, 2)].reshape(2 * BLK, HD)

    def pair_scores(keys, hs, shift):
        raw = mm(keys, qs[hs, :], NT) * SCALE2
        return jnp.where(shift >= low_ref[:, hs], raw, NEG)

    @pl.loop(1, HOPS + 1)
    def _(s):
        for which, buf in ((0, kbuf), (1, vbuf)):
            chain(buf, which, 0, 2 * s - 1, nxt).wait_recv()
            chain(buf, which, 0, 2 * s, prv).wait_recv()

            @pl.when(s < HOPS)
            def _(which=which, buf=buf):
                chain(buf, which, 2 * s - 1, 2 * s + 1, nxt).start()
                chain(buf, which, 2 * s, 2 * s + 2, prv).start()

        onehot(az, code_z, 96, s - 1)
        onehot(ax, code_x, 128, s - 1)
        onehot(azk, code_zk, 64, s - 1)
        onehot(axk, code_xk, 64, s - 1)
        keys = pair(kbuf, s)
        vals = pair(vbuf, s)
        shift = pair_shift(s)
        for hs in heads:
            s2 = pair_scores(keys, hs, shift)
            m_old = m_ref[:, hs]
            m = jnp.maximum(m_old, jnp.max(s2, axis=0, keepdims=True))
            p = jnp.exp2(s2 - m)
            fade = jnp.exp2(m_old - m)
            m_ref[:, hs] = m
            l_ref[:, hs] = l_ref[:, hs] * fade + jnp.sum(p, axis=0, keepdims=True)
            ot[:, hs] = ot[:, hs] * fade + mm(vals, p.astype(BF16), TN)

    take(3)
    for h, hs in enumerate(heads):
        grad = gin[:, h * HD : (h + 1) * HD]
        gs[hs, :] = grad
        mass = l_ref[:, hs]
        att = (ot[:, hs] / mass).astype(BF16)
        obf[:, hs] = att
        d_ref[:, hs] = jnp.sum(att.astype(F32) * grad.astype(F32).T, axis=0, keepdims=True)
        m_ref[:, hs] = m_ref[:, hs] + jnp.log2(mass)

    def z_copy(kind, src_z, dst_z):
        send, recv = ((zsend.at[0], zrecv.at[0]), (zsend.at[1], zrecv.at[1]), (zsend_k, zrecv_k))[kind]
        return pltpu.make_async_remote_copy(
            src_ref=send.at[dst_z],
            dst_ref=recv.at[src_z],
            send_sem=z_ss.at[kind, dst_z],
            recv_sem=z_rs.at[kind, src_z],
            device_id=(xi * ZN + dst_z, me),
            device_id_type=MESH,
        )

    def z_own(kind):
        send, recv = ((zsend.at[0], zrecv.at[0]), (zsend.at[1], zrecv.at[1]), (zsend_k, zrecv_k))[kind]
        return pltpu.make_async_copy(send.at[zi], recv.at[zi], loc_s.at[4 + kind])

    def x_copy(kind, src_x, dst_x):
        send, recv = ((xsend.at[0], xrecv.at[0]), (xsend.at[1], xrecv.at[1]), (xsend_k, xrecv_k))[kind]
        return pltpu.make_async_remote_copy(
            src_ref=send.at[dst_x],
            dst_ref=recv.at[:, src_x],
            send_sem=x_ss.at[kind, dst_x],
            recv_sem=x_rs.at[kind, src_x],
            device_id=(dst_x * ZN + zi, me),
            device_id_type=MESH,
        )

    def x_own(kind):
        send, recv = ((xsend.at[0], xrecv.at[0]), (xsend.at[1], xrecv.at[1]), (xsend_k, xrecv_k))[kind]
        return pltpu.make_async_copy(send.at[xi], recv.at[:, xi], loc_s.at[7 + kind])

    def z_start(kind):
        z_own(kind).start()

        @pl.loop(1, ZN)
        def _(i):
            z_copy(kind, zi, (zi + i) % ZN).start()

    def z_wait(kind):
        z_own(kind).wait()

        @pl.loop(1, ZN)
        def _(i):
            z_copy(kind, (zi + i) % ZN, (zi + i) % ZN).wait_recv()

    def x_start(kind):
        x_own(kind).start()

        @pl.loop(1, XN)
        def _(i):
            x_copy(kind, xi, (xi + i) % XN).start()

    def x_wait(kind):
        x_own(kind).wait()

        @pl.loop(1, XN)
        def _(i):
            x_copy(kind, (xi + i) % XN, (xi + i) % XN).wait_recv()

    def z_fill(kind, src):
        zsend[kind] = mm(az[...], src[...], NT).astype(BF16).reshape(ZN, ZR, HD)
        z_start(kind)

    def x_fill(kind):
        z_wait(kind)
        rows = zrecv[kind].reshape(ZN * ZR, HD)
        xsend[kind] = mm(ax[...], rows, NN).astype(BF16).reshape(XN, REP, 64, HD)
        x_start(kind)

    def finish(kind, out):
        x_wait(kind)
        for h in range(REP):
            out[:, h * HD : (h + 1) * HD] = mm(
                bfin[...], xrecv[kind, h].reshape(256, HD), NN
            ).astype(BF16)

    def back(side, which, s, to):
        return pltpu.make_async_remote_copy(
            src_ref=rs_send.at[s, side, which],
            dst_ref=rs_recv.at[s - 1, side, which],
            send_sem=rs_ss.at[s, side, which],
            recv_sem=rs_rs.at[s - 1, side, which],
            device_id=(to, me),
            device_id_type=MESH,
        )

    def back_wait(side, which, s):
        pltpu.make_async_remote_copy(
            src_ref=rs_send.at[s, side, which],
            dst_ref=rs_recv.at[s, side, which],
            send_sem=rs_ss.at[s, side, which],
            recv_sem=rs_rs.at[s, side, which],
            device_id=(nxt, me),
            device_id_type=MESH,
        ).wait_recv()

    def grads(s2, hs, keys, vals):
        p = jnp.exp2(s2 - m_ref[:, hs])
        dv = mm(p.astype(BF16), gs[hs, :], NN)
        dp = mm(vals, gs[hs, :], NT)
        ds = (p * (dp - d_ref[:, hs])).astype(BF16)
        dk = mm(ds, qs[hs, :], NN)
        return dk, dv, mm(keys, ds, TN)

    dqt[...] = jnp.zeros_like(dqt)

    @pl.loop(0, HOPS)
    def _(i):
        s = HOPS - i
        keys = pair(kbuf, s)
        vals = pair(vbuf, s)
        shift = pair_shift(s)
        dk = jnp.zeros((2 * BLK, HD), F32)
        dv = jnp.zeros((2 * BLK, HD), F32)
        for hs in heads:
            dk_h, dv_h, dq_h = grads(pair_scores(keys, hs, shift), hs, keys, vals)
            dk = dk + dk_h
            dv = dv + dv_h
            dqt[:, hs] += dq_h
        rs_part = (dk.reshape(2, BLK, HD), dv.reshape(2, BLK, HD))

        @pl.when(s == HOPS)
        def _():
            for which in range(2):
                for side in range(2):
                    rs_send[s, side, which] = rs_part[which][side].astype(BF16)

        @pl.when(s < HOPS)
        def _():
            for which in range(2):
                for side in range(2):
                    back_wait(side, which, s)
                    rs_send[s, side, which] = (
                        rs_part[which][side] + rs_recv[s, side, which].astype(F32)
                    ).astype(BF16)

        for which in range(2):
            back(0, which, s, prv).start()
            back(1, which, s, jnp.where(s == 1, down, nxt)).start()

        @pl.when(s == HOPS)
        def _():
            z_fill(0, obf)

        @pl.when(s == 2)
        def _():
            x_fill(0)

    dk = jnp.zeros((BLK, HD), F32)
    dv = jnp.zeros((BLK, HD), F32)
    for hs in heads:
        dk_h, dv_h, dq_h = grads(diag_scores(hs), hs, kbuf[0], vbuf[0])
        dk = dk + dk_h
        dv = dv + dv_h
        dqbf[:, hs] = ((dqt[:, hs] + dq_h) * SCALE).astype(BF16)
    z_fill(1, dqbf)
    for side in range(2):
        for which in range(2):
            back_wait(side, which, 0)
    dk = dk + rs_recv[0, 0, 0].astype(F32) + rs_recv[0, 1, 0].astype(F32)
    dv = dv + rs_recv[0, 0, 1].astype(F32) + rs_recv[0, 1, 1].astype(F32)
    rows = jnp.concatenate([(dk * SCALE).astype(BF16), dv.astype(BF16)], axis=0)
    zsend_k[...] = mm(azk[...], rows, NN).astype(BF16).reshape(ZN, ZK, HD)
    z_start(2)
    x_fill(1)
    z_wait(2)
    rows = zrecv_k[...].reshape(ZN * ZK, HD)
    xsend_k[...] = mm(axk[...], rows, NN).astype(BF16).reshape(XN, 2, 64, HD)
    x_start(2)
    finish(0, o_out)
    finish(1, dq_out)
    x_wait(2)
    dk_out[...] = mm(bfin[...], xrecv_k[0].reshape(256, HD), NN).astype(BF16)
    dv_out[...] = mm(bfin[...], xrecv_k[1].reshape(256, HD), NN).astype(BF16)

    for kind in range(4):

        @pl.loop(1, TP)
        def _(i, kind=kind):
            sent_piece(kind, (me + i) % TP).wait_send()

    @pl.loop(1, 2 * HOPS + 1)
    def _(pos):
        chain(kbuf, 0, 0, pos, nxt).wait_send()
        chain(vbuf, 1, 0, pos, nxt).wait_send()

    @pl.loop(1, HOPS + 1)
    def _(s):
        for side in range(2):
            for which in range(2):
                back(side, which, s, prv).wait_send()

    for kind in range(3):

        @pl.loop(1, ZN)
        def _(i, kind=kind):
            z_copy(kind, zi, (zi + i) % ZN).wait_send()

        @pl.loop(1, XN)
        def _(i, kind=kind):
            x_copy(kind, xi, (xi + i) % XN).wait_send()


def body(queries, keys, values, out_grad, doc_lengths, doc_groups):
    smem = pl.BlockSpec(memory_space=pltpu.SMEM)
    anywhere = pl.BlockSpec(memory_space=pl.ANY)
    vmem = pl.BlockSpec(memory_space=pltpu.VMEM)
    wide = REP * HD
    dma = pltpu.SemaphoreType.DMA
    return pl.pallas_call(
        kernel,
        out_shape=(
            jax.ShapeDtypeStruct((BLK, wide), BF16),
            jax.ShapeDtypeStruct((BLK, wide), BF16),
            jax.ShapeDtypeStruct((BLK, HD), BF16),
            jax.ShapeDtypeStruct((BLK, HD), BF16),
        ),
        in_specs=[smem, smem, anywhere, anywhere, anywhere, anywhere],
        out_specs=(vmem, vmem, vmem, vmem),
        scratch_shapes=[
            pltpu.VMEM((BLK, wide), BF16),
            pltpu.VMEM((BLK, wide), BF16),
            pltpu.VMEM((2 * HOPS + 1, BLK, HD), BF16),
            pltpu.VMEM((2 * HOPS + 1, BLK, HD), BF16),
            pltpu.VMEM((wide, HD), BF16),
            pltpu.VMEM((wide, HD), BF16),
            pltpu.VMEM((HD, wide), F32),
            pltpu.VMEM((HD, wide), BF16),
            pltpu.VMEM((1, wide), F32),
            pltpu.VMEM((1, wide), F32),
            pltpu.VMEM((1, wide), F32),
            pltpu.VMEM((HD, wide), F32),
            pltpu.VMEM((HD, wide), BF16),
            pltpu.VMEM((1, wide), jnp.int32),
            pltpu.VMEM((HOPS + 1, 2, 2, BLK, HD), BF16),
            pltpu.VMEM((HOPS + 1, 2, 2, BLK, HD), BF16),
            pltpu.VMEM((2, ZN, ZR, HD), BF16),
            pltpu.VMEM((2, ZN, ZR, HD), BF16),
            pltpu.VMEM((ZN, ZK, HD), BF16),
            pltpu.VMEM((ZN, ZK, HD), BF16),
            pltpu.VMEM((2, XN, REP, 64, HD), BF16),
            pltpu.VMEM((2, REP, XN, 64, HD), BF16),
            pltpu.VMEM((XN, 2, 64, HD), BF16),
            pltpu.VMEM((2, XN, 64, HD), BF16),
            pltpu.VMEM((ZN * ZR, wide), BF16),
            pltpu.VMEM((XN * 256, ZN * ZR), BF16),
            pltpu.VMEM((ZN * ZK, 2 * BLK), BF16),
            pltpu.VMEM((XN * 128, ZN * ZK), BF16),
            pltpu.VMEM((BLK, 256), BF16),
            pltpu.VMEM((1, wide), jnp.int32),
            pltpu.VMEM((1, ZN * ZR), jnp.int32),
            pltpu.VMEM((1, 2 * BLK), jnp.int32),
            pltpu.VMEM((1, ZN * ZK), jnp.int32),
            dma((4, TP)),
            dma((4, TP)),
            dma((2 * HOPS + 1, 2)),
            dma((2 * HOPS + 1, 2)),
            dma((HOPS + 1, 2, 2)),
            dma((HOPS + 1, 2, 2)),
            dma((3, ZN)),
            dma((3, ZN)),
            dma((3, XN)),
            dma((3, XN)),
            dma((10,)),
        ],
        compiler_params=pltpu.CompilerParams(
            collective_id=0, has_side_effects=True, vmem_limit_bytes=48 * 1024 * 1024
        ),
    )(doc_lengths, doc_groups, queries, keys, values, out_grad)


def solution(mesh):
    rows = P(("ctx", "tp"), None)
    in_specs = (rows, rows, rows, rows, P(), P())
    out_specs = (P("ctx", "tp"),) * 4
    return jax.shard_map(body, mesh=mesh, in_specs=in_specs, out_specs=out_specs, check_vma=False)
```

time: 662 us -> 130 us (0.20)
  the two profiles are of different devices: /device:TPU:34 before, /device:TPU:32 now
where the time goes in v1:
time: 130 us; the launch traced here: 129 us
  Pallas kernels  122 us (94%)
  local copies, waits for them, and re-layouts  7.17 us (6%)
    pallas_call x1, Pallas kernels, body(): pl.pallas_call(kernel, out_shape=(jax.ShapeDtypeStruct((BLK, wide), BF16)...  122 us
    unnamed x16, local copies, waits for them, and re-layouts  7.17 us

profile of v1, /device:TPU:32, one launch (start us, length us, event | category | flops | bytes accessed | tf_op | source)
XLA Modules:
  0.0 129.4 jit_solution(2717212788734858754)
XLA Ops:
  0.6 0.0 copy-start
  0.6 0.9 copy-done
  1.5 0.0 copy-start.1
  1.5 0.9 copy-done.1
  2.4 0.0 copy-start.2
  2.4 0.8 copy-done.2
  3.2 0.0 copy-start.3
  3.2 0.8 copy-done.3
  4.0 0.0 copy-start.4
  4.0 0.7 copy-done.4
  4.6 0.0 copy-start.5
  4.6 0.7 copy-done.5
  5.3 121.6 %shard_map.93 = (bf16[128,512]{1,0:T(8,128)(2,1)S(1)}, bf16[128,512]{1,0:T(8,128)(2,1)S(1)}, bf16[128,128]{1,0:T(8,128)(2,1)S(1)}, bf16[128,128]{1,0:T(8,128)(2,1)S(1)}) custom-call(s32[8]{0:T(128)S(1)} %copy-done.4, s32[8]{0:T(128)S(1)} %copy-done.5, bf16[16,4096]{1,0:T(8,128)(2,1)S(1)} %copy-done, bf16[16,1024]{1,0:T(8,128)(2,1)S(1)} %copy-done.2, ...), custom_call_target="tpu_custom_call" | custom-call | tf_op jit(solution)/shard_map/pallas_call | solution.py:503
  126.8 0.7 copy.14
  127.5 0.7 copy.15
  128.2 0.6 copy.16
  128.8 0.6 copy.17
Async XLA Ops:
  0.6 0.9 copy-start
  1.5 0.9 copy-start.1
  2.4 0.8 copy-start.2
  3.2 0.8 copy-start.3
  4.0 0.7 copy-start.4
  4.6 0.7 copy-start.5

commit v2 on v1

v2 whole, which is shorter than its diff:
```python
import jax
import jax.numpy as jnp
from jax import lax
from jax.experimental import pallas as pl
from jax.experimental.pallas import tpu as pltpu
from jax.sharding import PartitionSpec as P

HD = 128
REP = 4
BLK = 128
XN = 4
ZN = 16
CTX = XN * ZN
TP = 8
NDOC = 8
SUPS = 8
SCALE = HD ** (-0.5)
SCALE2 = SCALE * 1.4426950408889634
NEG = -1e30
ZR = 48
ZK = 32
MESH = pl.DeviceIdType.MESH
NT = (((1,), (1,)), ((), ()))
NN = (((1,), (0,)), ((), ()))
TN = (((0,), (0,)), ((), ()))
F32 = jnp.float32
BF16 = jnp.bfloat16


def mm(a, b, dims):
    return lax.dot_general(a, b, dims, preferred_element_type=F32)


def lane_iota(width):
    return lax.broadcasted_iota(jnp.int32, (1, width), 1)


def kernel(
    len_in, grp_in, q_in, k_in, v_in, g_in,
    o_out, dq_out, dk_out, dv_out,
    len_ref, grp_ref, qin, gin, kv, qs, gs, ot, obf, m_ref, l_ref, d_ref, dqt, dqbf, low_ref,
    keep, part, got, rs_send, rs_recv, zsend, zrecv, zsend_k, zrecv_k,
    xsend, xrecv, xsend_k, xrecv_k,
    az, ax, azk, axk, bfin, code_z, code_x, code_zk, code_xk,
    a_ss, a_rs, kv_ss, kv_rs, ag_ss, ag_rs, d_ss, d_rs, p_ss, p_rs, rs_ss, rs_rs,
    z_ss, z_rs, x_ss, x_rs, loc_s,
):
    c = lax.axis_index("ctx")
    me = lax.axis_index("tp")
    xi = c // ZN
    zi = c % ZN
    half = me % 2
    head = zi // 2
    sup = me // 2 * 2 + zi % 2
    row_block = 2 * sup + half
    here = xi * SUPS + sup
    twin = me + 1 - 2 * half

    def place(superblock, kv_head, core):
        j = superblock % SUPS
        return superblock // SUPS * ZN + 2 * kv_head + j % 2, j // 2 * 2 + core

    def ahead(steps):
        return place((here + steps + XN * SUPS) % (XN * SUPS), head, half)

    def input_to(kv_head, core):
        return place(xi * SUPS + zi // 2, kv_head, core)

    def input_from(core, piece):
        return xi * ZN + 2 * sup + core, piece

    def z_from(block):
        return place(xi * SUPS + block // 2, me, block % 2)

    barrier = pltpu.get_barrier_semaphore()

    def greet(ci, pi):
        pl.semaphore_signal(barrier, inc=1, device_id=(ci, pi), device_id_type=MESH)

    @pl.loop(0, TP)
    def _(i):
        for core in range(2):
            greet(*input_to(i, core))
            greet(*input_from(core, i))
        greet(*ahead(i + 1))
        greet(*ahead(-1 - i))

    @pl.loop(0, ZN)
    def _(i):
        greet(xi * ZN + i, head)
        greet(*z_from(i))

    @pl.loop(1, XN)
    def _(i):
        greet((xi + i) % XN * ZN + zi, me)

    greet(c, twin)
    pl.semaphore_wait(barrier, 6 * TP + 2 * ZN + XN - 1 + 1)

    pltpu.make_async_copy(len_in, len_ref, loc_s.at[0]).start()
    pltpu.make_async_copy(grp_in, grp_ref, loc_s.at[1]).start()

    def copy_to(src, dst, send_sem, recv_sem, to):
        return pltpu.make_async_remote_copy(
            src_ref=src,
            dst_ref=dst,
            send_sem=send_sem,
            recv_sem=recv_sem,
            device_id=to,
            device_id_type=MESH,
        )

    def start_to(src, dst, send_sem, recv_sem, to):
        is_self = (to[0] == c) & (to[1] == me)

        @pl.when(jnp.logical_not(is_self))
        def _():
            copy_to(src, dst, send_sem, recv_sem, to).start()

        @pl.when(is_self)
        def _():
            pltpu.make_async_copy(src, dst, recv_sem).start()

    def left(src, dst, send_sem, recv_sem, to):
        @pl.when((to[0] != c) | (to[1] != me))
        def _():
            copy_to(src, dst, send_sem, recv_sem, to).wait_send()

    def landed(dst, recv_sem):
        pltpu.make_async_copy(dst, dst, recv_sem).wait()

    def rows16(start):
        return pl.ds(pl.multiple_of(start, 16), 16)

    def lanes(kv_head, width):
        return pl.ds(pl.multiple_of(kv_head * width, width), width)

    def kv_piece(kind, kv_head, core):
        return (
            (k_in, v_in)[kind].at[:, lanes(kv_head, HD)],
            kv.at[kind, 0, rows16(zi % 2 * BLK + me * 16), :],
            kv_ss.at[kind, core, kv_head],
            kv_rs.at[kind, zi % 2, me],
            input_to(kv_head, core),
        )

    def wide_piece(kind, kv_head):
        return (
            (q_in, g_in)[kind].at[:, lanes(kv_head, REP * HD)],
            (qin, gin)[kind].at[rows16(me * 16), :],
            a_ss.at[kind, kv_head],
            a_rs.at[kind, me],
            input_to(kv_head, zi % 2),
        )

    @pl.loop(0, TP)
    def _(i):
        for kind in range(2):
            for core in range(2):
                start_to(*kv_piece(kind, (head + i) % TP, core))

    for kind in range(2):

        @pl.loop(0, TP)
        def _(i, kind=kind):
            start_to(*wide_piece(kind, (head + i) % TP))

    pltpu.make_async_copy(len_in, len_ref, loc_s.at[0]).wait()
    pltpu.make_async_copy(grp_in, grp_ref, loc_s.at[1]).wait()
    lens = [len_ref[d] for d in range(NDOC)]
    first = [1 - grp_ref[d] for d in range(NDOC)]
    starts = []
    total = jnp.int32(0)
    for d in range(NDOC):
        starts.append(total)
        total = total + lens[d]

    def count0(position):
        acc = 0
        for d in range(NDOC):
            acc = acc + first[d] * jnp.minimum(jnp.maximum(position - starts[d], 0), lens[d])
        return acc

    sbase = here * (2 * BLK)
    base = sbase + half * BLK
    jl = lane_iota(REP * BLK)
    tok = base + (jl & (BLK - 1))
    low = jnp.zeros_like(tok)
    for d in range(NDOC):
        low = jnp.maximum(low, jnp.where(tok >= starts[d], starts[d], 0))
    low_ref[...] = low - sbase

    def slot(tok, begin, size):
        r0 = count0(begin)
        c0 = (count0(begin + size) - r0 + 15) >> 4
        before = count0(tok)
        is0 = count0(tok + 1) - before == 1
        rank = jnp.where(is0, before, tok - before)
        k = jnp.where(is0, (rank - r0) >> 4, c0 + ((rank - begin + r0) >> 4))
        return rank & (ZN - 1), k

    zd, k = slot(tok, base, BLK)
    code_z[...] = zd * ZR + k * REP + (jl >> 7)
    zd, k = slot(sbase + lane_iota(2 * BLK), sbase, 2 * BLK)
    code_zk[...] = zd * ZK + k

    row0 = count0(xi * (ZN * BLK))
    row1 = xi * (ZN * BLK) - row0

    def arrived(number, size, k):
        begin = xi * (ZN * BLK) + number * size
        r0 = count0(begin)
        r0e = count0(begin + size)
        r1 = begin - r0
        r1e = begin + size - r0e
        c0 = (r0e - r0 + 15) >> 4
        g0 = k < c0
        kk = jnp.where(g0, k, k - c0)
        rb = jnp.where(g0, r0, r1)
        re = jnp.where(g0, r0e, r1e)
        rank = rb + ((zi - rb) & (ZN - 1)) + ZN * kk
        xd = jnp.where(g0, 0, 2) + ((rank >> 4) & 1)
        q = (rank - jnp.where(g0, row0, row1)) >> 5
        return rank < re, xd, q

    jx = lane_iota(ZN * ZR)
    zs = (jx * 43691) >> 21
    rem = jx - ZR * zs
    ok, xd, q = arrived(zs, BLK, rem >> 2)
    code_x[...] = jnp.where(ok, xd * 256 + (rem & 3) * 64 + q, -1)
    jk = lane_iota(ZN * ZK)
    ok, xd, q = arrived(jk >> 6, 2 * BLK, jk & (ZK - 1))
    code_xk[...] = jnp.where(ok, xd * 128 + ((jk >> 5) & 1) * 64 + q, -1)

    jf = lane_iota(4 * 64)
    xs = jf >> 6
    g1 = xi // 2
    res = (xi % 2) * ZN + zi
    rs0 = count0(xs * (ZN * BLK))
    rs0e = count0((xs + 1) * (ZN * BLK))
    rsb = jnp.where(g1 == 1, xs * (ZN * BLK) - rs0, rs0)
    rse = jnp.where(g1 == 1, (xs + 1) * (ZN * BLK) - rs0e, rs0e)
    rank = rsb + ((res - rsb) & 31) + 32 * (jf & 63)
    code = jnp.where(rank < rse, rank >> 5, -1)
    bfin[...] = jnp.where(
        lax.broadcasted_iota(jnp.int32, (BLK, 256), 0) == code, 1.0, 0.0
    ).astype(BF16)

    def onehot(dst, code, rows, step):
        begin = pl.multiple_of(step * rows, rows)
        ids = begin + lax.broadcasted_iota(jnp.int32, (rows, dst.shape[1]), 0)
        dst[pl.ds(begin, rows), :] = jnp.where(ids == code[...], 1.0, 0.0).astype(BF16)

    @pl.loop(0, TP)
    def _(i):
        for kind in range(2):
            for core in range(2):
                landed(kv.at[kind, 0, rows16(core * BLK + i * 16), :], kv_rs.at[kind, core, i])

    def gather(r):
        return copy_to(kv.at[half, 0], kv.at[half, r], ag_ss.at[r], ag_rs.at[r], ahead(r))

    def across(r):
        return copy_to(kv.at[half, r], kv.at[half, r], d_ss.at[r], d_rs.at[r], (c, twin))

    def take(r):
        landed(kv.at[half, r], ag_rs.at[r])
        across(r).start()

    @pl.loop(1, SUPS + 1)
    def _(r):
        gather(r).start()

    def wide_landed(kind):
        @pl.loop(0, TP)
        def _(i):
            landed((qin, gin)[kind].at[rows16(i * 16), :], a_rs.at[kind, i])

    wide_landed(0)
    for h in range(REP):
        qs[h * BLK : (h + 1) * BLK, :] = qin[:, h * HD : (h + 1) * HD]

    heads = [slice(h * BLK, (h + 1) * BLK) for h in range(REP)]
    m_ref[...] = jnp.full_like(m_ref, NEG)
    l_ref[...] = jnp.zeros_like(l_ref)
    ot[...] = jnp.zeros_like(ot)

    def scores(r, hs):
        raw = mm(kv[0, r], qs[hs, :], NT) * SCALE2
        place_in = lax.broadcasted_iota(jnp.int32, (2 * BLK, BLK), 0) - 2 * BLK * r
        query = lax.broadcasted_iota(jnp.int32, (2 * BLK, BLK), 1) + half * BLK
        return jnp.where((place_in <= query) & (place_in >= low_ref[:, hs]), raw, NEG)

    def forward(r):
        for hs in heads:
            s2 = scores(r, hs)
            m_old = m_ref[:, hs]
            m = jnp.maximum(m_old, jnp.max(s2, axis=0, keepdims=True))
            p = jnp.exp2(s2 - m)
            fade = jnp.exp2(m_old - m)
            m_ref[:, hs] = m
            l_ref[:, hs] = l_ref[:, hs] * fade + jnp.sum(p, axis=0, keepdims=True)
            ot[:, hs] = ot[:, hs] * fade + mm(kv[1, r], p.astype(BF16), TN)

    def tables(step):
        onehot(az, code_z, 96, step)
        onehot(ax, code_x, 128, step)
        onehot(azk, code_zk, 64, step)
        onehot(axk, code_xk, 64, step)

    forward(0)

    @pl.loop(0, SUPS)
    def _(step):
        tables(step)

    take(1)

    @pl.loop(1, SUPS + 1)
    def _(r):
        @pl.when(r < SUPS)
        def _():
            take(r + 1)

        landed(kv.at[1 - half, r], d_rs.at[r])
        forward(r)

    wide_landed(1)
    for h, hs in enumerate(heads):
        grad = gin[:, h * HD : (h + 1) * HD]
        gs[hs, :] = grad
        mass = l_ref[:, hs]
        att = (ot[:, hs] / mass).astype(BF16)
        obf[:, hs] = att
        d_ref[:, hs] = jnp.sum(att.astype(F32) * grad.astype(F32).T, axis=0, keepdims=True)
        m_ref[:, hs] = m_ref[:, hs] + jnp.log2(mass)

    zbuf = ((zsend.at[0], zrecv.at[0]), (zsend.at[1], zrecv.at[1]), (zsend_k, zrecv_k))
    xbuf = ((xsend.at[0], xrecv.at[0]), (xsend.at[1], xrecv.at[1]), (xsend_k, xrecv_k))

    def z_move(kind, dst_z):
        send, recv = zbuf[kind]
        return (
            send.at[dst_z],
            recv.at[row_block],
            z_ss.at[kind, dst_z],
            z_rs.at[kind, row_block],
            (xi * ZN + dst_z, head),
        )

    def x_move(kind, dst_x):
        send, recv = xbuf[kind]
        return (
            send.at[dst_x],
            recv.at[:, xi],
            x_ss.at[kind, dst_x],
            x_rs.at[kind, xi],
            (dst_x * ZN + zi, me),
        )

    def z_start(kind):
        @pl.loop(0, ZN)
        def _(i):
            start_to(*z_move(kind, (zi + i) % ZN))

    def z_wait(kind):
        @pl.loop(0, ZN)
        def _(i):
            landed(zbuf[kind][1].at[i], z_rs.at[kind, i])

    def x_start(kind):
        @pl.loop(0, XN)
        def _(i):
            start_to(*x_move(kind, (xi + i) % XN))

    def x_wait(kind):
        @pl.loop(0, XN)
        def _(i):
            landed(xbuf[kind][1].at[:, i], x_rs.at[kind, i])

    def z_fill(kind, src):
        zsend[kind] = mm(az[...], src[...], NT).astype(BF16).reshape(ZN, ZR, HD)
        z_start(kind)

    def x_fill(kind):
        z_wait(kind)
        rows = zrecv[kind].reshape(ZN * ZR, HD)
        xsend[kind] = mm(ax[...], rows, NN).astype(BF16).reshape(XN, REP, 64, HD)
        x_start(kind)

    def finish(kind, out):
        x_wait(kind)
        for h in range(REP):
            out[:, h * HD : (h + 1) * HD] = mm(
                bfin[...], xrecv[kind, h].reshape(256, HD), NN
            ).astype(BF16)

    def to_twin(r):
        return copy_to(part.at[r], got.at[r], p_ss.at[r], p_rs.at[r], (c, twin))

    def to_owner(r):
        return copy_to(rs_send.at[r], rs_recv.at[r], rs_ss.at[r], rs_rs.at[r], ahead(-r))

    def both_cores(r):
        landed(got.at[r], p_rs.at[r])
        return keep[r] + got[r].astype(F32)

    dqt[...] = jnp.zeros_like(dqt)

    @pl.loop(0, SUPS + 1)
    def _(i):
        r = SUPS - i
        dk = jnp.zeros((2 * BLK, HD), F32)
        dv = jnp.zeros((2 * BLK, HD), F32)
        for hs in heads:
            p = jnp.exp2(scores(r, hs) - m_ref[:, hs])
            dv = dv + mm(p.astype(BF16), gs[hs, :], NN)
            dp = mm(kv[1, r], gs[hs, :], NT)
            ds = (p * (dp - d_ref[:, hs])).astype(BF16)
            dk = dk + mm(ds, qs[hs, :], NN)
            dqt[:, hs] += mm(kv[0, r], ds, TN)
        keep[r] = jnp.where(half == 0, dk, dv)
        part[r] = jnp.where(half == 0, dv, dk).astype(BF16)
        to_twin(r).start()

        @pl.when(r < SUPS)
        def _():
            rs_send[r + 1] = both_cores(r + 1).astype(BF16)
            to_owner(r + 1).start()

        @pl.when(r == SUPS)
        def _():
            z_fill(0, obf)

    dqbf[...] = (dqt[...] * SCALE).astype(BF16)
    z_fill(1, dqbf)
    x_fill(0)
    terms = both_cores(0)
    for r in range(1, SUPS + 1):
        landed(rs_recv.at[r], rs_rs.at[r])
        terms = terms + rs_recv[r].astype(F32)
    rows = (terms * jnp.where(half == 0, SCALE, 1.0)).astype(BF16)
    zsend_k[...] = mm(azk[...], rows, NN).astype(BF16).reshape(ZN, ZK, HD)
    z_start(2)
    x_fill(1)
    finish(0, o_out)
    z_wait(2)
    rows = zrecv_k[...].reshape(ZN * ZK, HD)
    xsend_k[...] = mm(axk[...], rows, NN).astype(BF16).reshape(XN, 2, 64, HD)
    x_start(2)
    finish(1, dq_out)
    x_wait(2)
    dk_out[...] = mm(bfin[...], xrecv_k[0].reshape(256, HD), NN).astype(BF16)
    dv_out[...] = mm(bfin[...], xrecv_k[1].reshape(256, HD), NN).astype(BF16)

    @pl.loop(0, TP)
    def _(i):
        for kind in range(2):
            left(*wide_piece(kind, i))
            for core in range(2):
                left(*kv_piece(kind, i, core))

    @pl.loop(1, SUPS + 1)
    def _(r):
        gather(r).wait_send()
        across(r).wait_send()
        to_twin(r).wait_send()
        to_owner(r).wait_send()

    to_twin(0).wait_send()
    for kind in range(3):

        @pl.loop(0, ZN)
        def _(i, kind=kind):
            left(*z_move(kind, i))

        @pl.loop(0, XN)
        def _(i, kind=kind):
            left(*x_move(kind, i))


def body(queries, keys, values, out_grad, doc_lengths, doc_groups):
    anywhere = pl.BlockSpec(memory_space=pl.ANY)
    vmem = pl.BlockSpec(memory_space=pltpu.VMEM)
    wide = REP * HD
    dma = pltpu.SemaphoreType.DMA
    return pl.pallas_call(
        kernel,
        out_shape=(
            jax.ShapeDtypeStruct((BLK, wide), BF16),
            jax.ShapeDtypeStruct((BLK, wide), BF16),
            jax.ShapeDtypeStruct((BLK, HD), BF16),
            jax.ShapeDtypeStruct((BLK, HD), BF16),
        ),
        in_specs=[anywhere] * 6,
        out_specs=(vmem, vmem, vmem, vmem),
        scratch_shapes=[
            pltpu.SMEM((NDOC,), jnp.int32),
            pltpu.SMEM((NDOC,), jnp.int32),
            pltpu.VMEM((BLK, wide), BF16),
            pltpu.VMEM((BLK, wide), BF16),
            pltpu.VMEM((2, SUPS + 1, 2 * BLK, HD), BF16),
            pltpu.VMEM((wide, HD), BF16),
            pltpu.VMEM((wide, HD), BF16),
            pltpu.VMEM((HD, wide), F32),
            pltpu.VMEM((HD, wide), BF16),
            pltpu.VMEM((1, wide), F32),
            pltpu.VMEM((1, wide), F32),
            pltpu.VMEM((1, wide), F32),
            pltpu.VMEM((HD, wide), F32),
            pltpu.VMEM((HD, wide), BF16),
            pltpu.VMEM((1, wide), jnp.int32),
            pltpu.VMEM((SUPS + 1, 2 * BLK, HD), F32),
            pltpu.VMEM((SUPS + 1, 2 * BLK, HD), BF16),
            pltpu.VMEM((SUPS + 1, 2 * BLK, HD), BF16),
            pltpu.VMEM((SUPS + 1, 2 * BLK, HD), BF16),
            pltpu.VMEM((SUPS + 1, 2 * BLK, HD), BF16),
            pltpu.VMEM((2, ZN, ZR, HD), BF16),
            pltpu.VMEM((2, ZN, ZR, HD), BF16),
            pltpu.VMEM((ZN, ZK, HD), BF16),
            pltpu.VMEM((ZN, ZK, HD), BF16),
            pltpu.VMEM((2, XN, REP, 64, HD), BF16),
            pltpu.VMEM((2, REP, XN, 64, HD), BF16),
            pltpu.VMEM((XN, 2, 64, HD), BF16),
            pltpu.VMEM((2, XN, 64, HD), BF16),
            pltpu.VMEM((ZN * ZR, wide), BF16),
            pltpu.VMEM((XN * 256, ZN * ZR), BF16),
            pltpu.VMEM((ZN * ZK, 2 * BLK), BF16),
            pltpu.VMEM((XN * 128, ZN * ZK), BF16),
            pltpu.VMEM((BLK, 256), BF16),
            pltpu.VMEM((1, wide), jnp.int32),
            pltpu.VMEM((1, ZN * ZR), jnp.int32),
            pltpu.VMEM((1, 2 * BLK), jnp.int32),
            pltpu.VMEM((1, ZN * ZK), jnp.int32),
            dma((2, TP)),
            dma((2, TP)),
            dma((2, 2, TP)),
            dma((2, 2, TP)),
            dma((SUPS + 1,)),
            dma((SUPS + 1,)),
            dma((SUPS + 1,)),
            dma((SUPS + 1,)),
            dma((SUPS + 1,)),
            dma((SUPS + 1,)),
            dma((SUPS + 1,)),
            dma((SUPS + 1,)),
            dma((3, ZN)),
            dma((3, ZN)),
            dma((3, XN)),
            dma((3, XN)),
            dma((2,)),
        ],
        compiler_params=pltpu.CompilerParams(
            collective_id=0, has_side_effects=True, vmem_limit_bytes=60 * 1024 * 1024
        ),
    )(doc_lengths, doc_groups, queries, keys, values, out_grad)


def solution(mesh):
    rows = P(("ctx", "tp"), None)
    in_specs = (rows, rows, rows, rows, P(), P())
    out_specs = (P("ctx", "tp"),) * 4
    return jax.shard_map(body, mesh=mesh, in_specs=in_specs, out_specs=out_specs, check_vma=False)
```

time: 130 us -> 98.2 us (0.76)
  the two profiles are of different devices: /device:TPU:32 before, /device:TPU:16 now
where the time goes in v2:
time: 98.2 us; the launch traced here: 97.9 us
  Pallas kernels  93.5 us (95%)
  local copies, waits for them, and re-layouts  3.75 us (4%)
    pallas_call x1, Pallas kernels, body(): pl.pallas_call(kernel, out_shape=(jax.ShapeDtypeStruct((BLK, wide), BF16)...  93.5 us
    unnamed x10, local copies, waits for them, and re-layouts  3.75 us

profile of v2, /device:TPU:16, one launch (start us, length us, event | category | flops | bytes accessed | tf_op | source)
XLA Modules:
  0.0 97.9 jit_solution(14711577862668044029)
XLA Ops:
  0.6 93.5 %shard_map.93 = (bf16[128,512]{1,0:T(8,128)(2,1)}, bf16[128,512]{1,0:T(8,128)(2,1)}, bf16[128,128]{1,0:T(8,128)(2,1)}, bf16[128,128]{1,0:T(8,128)(2,1)}) custom-call(s32[8]{0:T(128)} %len_in.1, s32[8]{0:T(128)} %grp_in.1, bf16[16,4096]{1,0:T(8,128)(2,1)} %q_in.1, bf16[16,1024]{1,0:T(8,128)(2,1)} %k_in.1, bf16[16,1024]{1,0:T(8,128)(2,1)} %v_in.1, ...), custom_call_target="tpu_custom_call" | custom-call | tf_op jit(solution)/shard_map/pallas_call | solution.py:487
  94.1 0.0 copy-start
  94.1 1.6 %copy.14 = bf16[128,512]{1,0:T(8,128)(2,1)} copy(bf16[128,512]{1,0:T(8,128)(2,1)} %get-tuple-element.8) | data formatting | bytes 262144
  95.7 0.0 copy-done
  95.7 0.0 copy-start.2
  95.7 0.7 copy.15
  96.4 0.1 copy-done.2
  96.5 0.0 copy-start.1
  96.5 0.6 copy.16
  97.1 0.2 copy-done.1
  97.3 0.6 copy.17
Async XLA Ops:
  94.1 1.6 %copy-start = (bf16[128,512]{1,0:T(8,128)(2,1)S(1)}, bf16[128,512]{1,0:T(8,128)(2,1)}, u32[]{:S(2)}) copy-start(bf16[128,512]{1,0:T(8,128)(2,1)} %get-tuple-element.9) | copy-start | bytes 393220
  95.7 0.8 copy-start.2
  96.5 0.8 copy-start.1

commit v3 on v2

--- a/solution.py
+++ b/solution.py
@@ -135,13 +135,13 @@
     def lanes(kv_head, width):
         return pl.ds(pl.multiple_of(kv_head * width, width), width)
 
-    def kv_piece(kind, kv_head, core):
+    def kv_piece(kind, kv_head):
         return (
             (k_in, v_in)[kind].at[:, lanes(kv_head, HD)],
             kv.at[kind, 0, rows16(zi % 2 * BLK + me * 16), :],
-            kv_ss.at[kind, core, kv_head],
-            kv_rs.at[kind, zi % 2, me],
-            input_to(kv_head, core),
+            kv_ss.at[kind, kv_head],
+            kv_rs.at[zi % 2, me],
+            input_to(kv_head, kind),
         )
 
     def wide_piece(kind, kv_head):
@@ -156,8 +156,7 @@
     @pl.loop(0, TP)
     def _(i):
         for kind in range(2):
-            for core in range(2):
-                start_to(*kv_piece(kind, (head + i) % TP, core))
+            start_to(*kv_piece(kind, (head + i) % TP))
 
     for kind in range(2):
 
@@ -251,11 +250,17 @@
         ids = begin + lax.broadcasted_iota(jnp.int32, (rows, dst.shape[1]), 0)
         dst[pl.ds(begin, rows), :] = jnp.where(ids == code[...], 1.0, 0.0).astype(BF16)
 
+    @pl.loop(0, SUPS)
+    def _(step):
+        onehot(az, code_z, 96, step)
+        onehot(ax, code_x, 128, step)
+        onehot(azk, code_zk, 64, step)
+        onehot(axk, code_xk, 64, step)
+
     @pl.loop(0, TP)
     def _(i):
-        for kind in range(2):
-            for core in range(2):
-                landed(kv.at[kind, 0, rows16(core * BLK + i * 16), :], kv_rs.at[kind, core, i])
+        for core in range(2):
+            landed(kv.at[half, 0, rows16(core * BLK + i * 16), :], kv_rs.at[core, i])
 
     def gather(r):
         return copy_to(kv.at[half, 0], kv.at[half, r], ag_ss.at[r], ag_rs.at[r], ahead(r))
@@ -270,6 +275,8 @@
     @pl.loop(1, SUPS + 1)
     def _(r):
         gather(r).start()
+
+    across(0).start()
 
     def wide_landed(kind):
         @pl.loop(0, TP)
@@ -302,18 +309,8 @@
             l_ref[:, hs] = l_ref[:, hs] * fade + jnp.sum(p, axis=0, keepdims=True)
             ot[:, hs] = ot[:, hs] * fade + mm(kv[1, r], p.astype(BF16), TN)
 
-    def tables(step):
-        onehot(az, code_z, 96, step)
-        onehot(ax, code_x, 128, step)
-        onehot(azk, code_zk, 64, step)
-        onehot(axk, code_xk, 64, step)
-
+    landed(kv.at[1 - half, 0], d_rs.at[0])
     forward(0)
-
-    @pl.loop(0, SUPS)
-    def _(step):
-        tables(step)
-
     take(1)
 
     @pl.loop(1, SUPS + 1)
@@ -457,8 +454,7 @@
     def _(i):
         for kind in range(2):
             left(*wide_piece(kind, i))
-            for core in range(2):
-                left(*kv_piece(kind, i, core))
+            left(*kv_piece(kind, i))
 
     @pl.loop(1, SUPS + 1)
     def _(r):
@@ -467,6 +463,7 @@
         to_twin(r).wait_send()
         to_owner(r).wait_send()
 
+    across(0).wait_send()
     to_twin(0).wait_send()
     for kind in range(3):
 
@@ -534,8 +531,8 @@
             pltpu.VMEM((1, ZN * ZK), jnp.int32),
             dma((2, TP)),
             dma((2, TP)),
-            dma((2, 2, TP)),
-            dma((2, 2, TP)),
+            dma((2, TP)),
+            dma((2, TP)),
             dma((SUPS + 1,)),
             dma((SUPS + 1,)),
             dma((SUPS + 1,)),

time: 98.2 us -> 92.4 us (0.941)
  the two profiles are of different devices: /device:TPU:16 before, /device:TPU:9 now
where the time goes in v3:
time: 92.4 us; the launch traced here: 92.1 us
  Pallas kernels  87.7 us (95%)
  local copies, waits for them, and re-layouts  3.75 us (4%)
    pallas_call x1, Pallas kernels, body(): pl.pallas_call(kernel, out_shape=(jax.ShapeDtypeStruct((BLK, wide), BF16)...  87.7 us
    unnamed x10, local copies, waits for them, and re-layouts  3.75 us

profile of v3, /device:TPU:9, one launch (start us, length us, event | category | flops | bytes accessed | tf_op | source)
XLA Modules:
  0.0 92.1 jit_solution(6622880450555337828)
XLA Ops:
  0.6 87.7 %shard_map.93 = (bf16[128,512]{1,0:T(8,128)(2,1)}, bf16[128,512]{1,0:T(8,128)(2,1)}, bf16[128,128]{1,0:T(8,128)(2,1)}, bf16[128,128]{1,0:T(8,128)(2,1)}) custom-call(s32[8]{0:T(128)} %len_in.1, s32[8]{0:T(128)} %grp_in.1, bf16[16,4096]{1,0:T(8,128)(2,1)} %q_in.1, bf16[16,1024]{1,0:T(8,128)(2,1)} %k_in.1, bf16[16,1024]{1,0:T(8,128)(2,1)} %v_in.1, ...), custom_call_target="tpu_custom_call" | custom-call | tf_op jit(solution)/shard_map/pallas_call | solution.py:484
  88.3 0.0 copy-start
  88.4 1.6 %copy.14 = bf16[128,512]{1,0:T(8,128)(2,1)} copy(bf16[128,512]{1,0:T(8,128)(2,1)} %get-tuple-element.8) | data formatting | bytes 262144
  90.0 0.0 copy-done
  90.0 0.0 copy-start.2
  90.0 0.7 copy.15
  90.6 0.1 copy-done.2
  90.7 0.0 copy-start.1
  90.7 0.6 copy.16
  91.3 0.2 copy-done.1
  91.5 0.6 copy.17
Async XLA Ops:
  88.3 1.6 %copy-start = (bf16[128,512]{1,0:T(8,128)(2,1)S(1)}, bf16[128,512]{1,0:T(8,128)(2,1)}, u32[]{:S(2)}) copy-start(bf16[128,512]{1,0:T(8,128)(2,1)} %get-tuple-element.9) | copy-start | bytes 393220
  90.0 0.8 copy-start.2
  90.7 0.8 copy-start.1

commit v4 on v3

--- a/solution.py
+++ b/solution.py
@@ -14,10 +14,12 @@
 TP = 8
 NDOC = 8
 SUPS = 8
+EXTRA = 17
+PLANES = 3
 SCALE = HD ** (-0.5)
 SCALE2 = SCALE * 1.4426950408889634
 NEG = -1e30
-ZR = 48
+ZR = 32
 ZK = 32
 MESH = pl.DeviceIdType.MESH
 NT = (((1,), (1,)), ((), ()))
@@ -37,11 +39,11 @@
 
 def kernel(
     len_in, grp_in, q_in, k_in, v_in, g_in,
-    o_out, dq_out, dk_out, dv_out,
+    xrecv, xrecv_k, bfin, code_f,
     len_ref, grp_ref, qin, gin, kv, qs, gs, ot, obf, m_ref, l_ref, d_ref, dqt, dqbf, low_ref,
     keep, part, got, rs_send, rs_recv, zsend, zrecv, zsend_k, zrecv_k,
-    xsend, xrecv, xsend_k, xrecv_k,
-    az, ax, azk, axk, bfin, code_z, code_x, code_zk, code_xk,
+    xsend, xsend_k,
+    az, ax, azk, axk, aze, extra, code_z, code_e, code_x, code_zk, code_xk,
     a_ss, a_rs, kv_ss, kv_rs, ag_ss, ag_rs, d_ss, d_rs, p_ss, p_rs, rs_ss, rs_rs,
     z_ss, z_rs, x_ss, x_rs, loc_s,
 ):
@@ -129,6 +131,9 @@
     def landed(dst, recv_sem):
         pltpu.make_async_copy(dst, dst, recv_sem).wait()
 
+    def far_first(t, size):
+        return jnp.where(t % 2 == 1, size // 2 - (t + 1) // 2, size // 2 + t // 2)
+
     def rows16(start):
         return pl.ds(pl.multiple_of(start, 16), 16)
 
@@ -156,13 +161,13 @@
     @pl.loop(0, TP)
     def _(i):
         for kind in range(2):
-            start_to(*kv_piece(kind, (head + i) % TP))
+            start_to(*kv_piece(kind, (head + far_first(i, TP)) % TP))
 
     for kind in range(2):
 
         @pl.loop(0, TP)
         def _(i, kind=kind):
-            start_to(*wide_piece(kind, (head + i) % TP))
+            start_to(*wide_piece(kind, (head + far_first(i, TP)) % TP))
 
     pltpu.make_async_copy(len_in, len_ref, loc_s.at[0]).wait()
     pltpu.make_async_copy(grp_in, grp_ref, loc_s.at[1]).wait()
@@ -199,7 +204,8 @@
         return rank & (ZN - 1), k
 
     zd, k = slot(tok, base, BLK)
-    code_z[...] = zd * ZR + k * REP + (jl >> 7)
+    code_z[...] = jnp.where(k < 8, zd * ZR + k * REP + (jl >> 7), -1)
+    code_e[...] = jnp.where(k < 8, -REP - 1, zd * ZK + EXTRA + (jl >> 7))
     zd, k = slot(sbase + lane_iota(2 * BLK), sbase, 2 * BLK)
     code_zk[...] = zd * ZK + k
 
@@ -223,13 +229,19 @@
         return rank < re, xd, q
 
     jx = lane_iota(ZN * ZR)
-    zs = (jx * 43691) >> 21
-    rem = jx - ZR * zs
-    ok, xd, q = arrived(zs, BLK, rem >> 2)
-    code_x[...] = jnp.where(ok, xd * 256 + (rem & 3) * 64 + q, -1)
+    ok, xd, q = arrived(jx >> 5, BLK, (jx & (ZR - 1)) >> 2)
+    code_x[...] = jnp.where(ok, xd * 256 + (jx & 3) * 64 + q, -1)
     jk = lane_iota(ZN * ZK)
     ok, xd, q = arrived(jk >> 6, 2 * BLK, jk & (ZK - 1))
-    code_xk[...] = jnp.where(ok, xd * 128 + ((jk >> 5) & 1) * 64 + q, -1)
+    in_pair = jnp.where(ok, xd * 192 + ((jk >> 5) & 1) * 64 + q, -1)
+    row = jk & (ZK - 1)
+    begin = xi * (ZN * BLK) + (jk >> 5) * BLK
+    holder = 0
+    for d in range(1, NDOC):
+        holder = holder + jnp.where(starts[d] <= begin, 1, 0)
+    ok, xd, _ = arrived(jk >> 5, BLK, jnp.full_like(jk, 8))
+    ninth = jnp.where(ok & (row < EXTRA + 8), xd * 192 + 128 + holder * 8 + row - EXTRA, -1)
+    code_xk[...] = jnp.where(row < EXTRA, in_pair, ninth)
 
     jf = lane_iota(4 * 64)
     xs = jf >> 6
@@ -245,17 +257,35 @@
         lax.broadcasted_iota(jnp.int32, (BLK, 256), 0) == code, 1.0, 0.0
     ).astype(BF16)
 
-    def onehot(dst, code, rows, step):
+    xs = jf >> 6
+    holder = (jf >> 3) & 7
+    this_start = 0
+    next_start = 0
+    for d in range(NDOC - 1):
+        this_start = this_start + jnp.where(holder == d, starts[d], 0)
+        next_start = next_start + jnp.where(holder == d, starts[d + 1], 0)
+    begin = ((next_start - 1) >> 7) << 7
+    r0 = count0(begin)
+    r0e = count0(begin + BLK)
+    rank = begin - r0
+    rank = rank + ((zi - rank) & (ZN - 1)) + ZN * (8 - ((r0e - r0 + 15) >> 4))
+    ok = (holder < NDOC - 1) & (this_start <= begin) & ((begin >> 11) == xs)
+    ok = ok & (rank < begin + BLK - r0e) & (2 + ((rank >> 4) & 1) == xi)
+    code_f[...] = jnp.where(ok, rank >> 5, -1)
+
+    def onehot(dst, code, rows, step, shift=0):
         begin = pl.multiple_of(step * rows, rows)
-        ids = begin + lax.broadcasted_iota(jnp.int32, (rows, dst.shape[1]), 0)
+        ids = begin - shift + lax.broadcasted_iota(jnp.int32, (rows, dst.shape[1]), 0)
         dst[pl.ds(begin, rows), :] = jnp.where(ids == code[...], 1.0, 0.0).astype(BF16)
 
     @pl.loop(0, SUPS)
     def _(step):
-        onehot(az, code_z, 96, step)
+        onehot(az, code_z, 64, step)
+        onehot(aze.at[0], code_e, 64, step)
+        onehot(aze.at[1], code_e, 64, step, REP)
         onehot(ax, code_x, 128, step)
         onehot(azk, code_zk, 64, step)
-        onehot(axk, code_xk, 64, step)
+        onehot(axk, code_xk, 96, step)
 
     @pl.loop(0, TP)
     def _(i):
@@ -272,9 +302,15 @@
         landed(kv.at[half, r], ag_rs.at[r])
         across(r).start()
 
-    @pl.loop(1, SUPS + 1)
-    def _(r):
-        gather(r).start()
+    def crossing_first(t):
+        return t + 1
+
+    def crossing_last(t):
+        return jnp.where(t < SUPS // 2, 2 * t + 2, 2 * t + 1 - SUPS)
+
+    @pl.loop(0, SUPS)
+    def _(t):
+        gather(crossing_first(t)).start()
 
     across(0).start()
 
@@ -288,18 +324,19 @@
         qs[h * BLK : (h + 1) * BLK, :] = qin[:, h * HD : (h + 1) * HD]
 
     heads = [slice(h * BLK, (h + 1) * BLK) for h in range(REP)]
+    pairs = [slice(h * BLK, (h + 2) * BLK) for h in range(0, REP, 2)]
     m_ref[...] = jnp.full_like(m_ref, NEG)
     l_ref[...] = jnp.zeros_like(l_ref)
     ot[...] = jnp.zeros_like(ot)
 
     def scores(r, hs):
         raw = mm(kv[0, r], qs[hs, :], NT) * SCALE2
-        place_in = lax.broadcasted_iota(jnp.int32, (2 * BLK, BLK), 0) - 2 * BLK * r
-        query = lax.broadcasted_iota(jnp.int32, (2 * BLK, BLK), 1) + half * BLK
+        place_in = lax.broadcasted_iota(jnp.int32, raw.shape, 0) - 2 * BLK * r
+        query = (lax.broadcasted_iota(jnp.int32, raw.shape, 1) & (BLK - 1)) + half * BLK
         return jnp.where((place_in <= query) & (place_in >= low_ref[:, hs]), raw, NEG)
 
     def forward(r):
-        for hs in heads:
+        for hs in pairs:
             s2 = scores(r, hs)
             m_old = m_ref[:, hs]
             m = jnp.maximum(m_old, jnp.max(s2, axis=0, keepdims=True))
@@ -311,14 +348,15 @@
 
     landed(kv.at[1 - half, 0], d_rs.at[0])
     forward(0)
-    take(1)
-
-    @pl.loop(1, SUPS + 1)
-    def _(r):
-        @pl.when(r < SUPS)
+    take(crossing_last(0))
+
+    @pl.loop(0, SUPS)
+    def _(t):
+        @pl.when(t < SUPS - 1)
         def _():
-            take(r + 1)
-
+            take(crossing_last(t + 1))
+
+        r = crossing_last(t)
         landed(kv.at[1 - half, r], d_rs.at[r])
         forward(r)
 
@@ -358,7 +396,7 @@
     def z_start(kind):
         @pl.loop(0, ZN)
         def _(i):
-            start_to(*z_move(kind, (zi + i) % ZN))
+            start_to(*z_move(kind, (zi + far_first(i, ZN)) % ZN))
 
     def z_wait(kind):
         @pl.loop(0, ZN)
@@ -378,6 +416,7 @@
     def z_fill(kind, src):
         zsend[kind] = mm(az[...], src[...], NT).astype(BF16).reshape(ZN, ZR, HD)
         z_start(kind)
+        extra[kind] = mm(aze[kind], src[...], NT)
 
     def x_fill(kind):
         z_wait(kind)
@@ -385,13 +424,6 @@
         xsend[kind] = mm(ax[...], rows, NN).astype(BF16).reshape(XN, REP, 64, HD)
         x_start(kind)
 
-    def finish(kind, out):
-        x_wait(kind)
-        for h in range(REP):
-            out[:, h * HD : (h + 1) * HD] = mm(
-                bfin[...], xrecv[kind, h].reshape(256, HD), NN
-            ).astype(BF16)
-
     def to_twin(r):
         return copy_to(part.at[r], got.at[r], p_ss.at[r], p_rs.at[r], (c, twin))
 
@@ -403,13 +435,14 @@
         return keep[r] + got[r].astype(F32)
 
     dqt[...] = jnp.zeros_like(dqt)
+    z_fill(0, obf)
 
     @pl.loop(0, SUPS + 1)
     def _(i):
-        r = SUPS - i
+        r = jnp.where(i < SUPS, crossing_first(i), 0)
         dk = jnp.zeros((2 * BLK, HD), F32)
         dv = jnp.zeros((2 * BLK, HD), F32)
-        for hs in heads:
+        for hs in pairs:
             p = jnp.exp2(scores(r, hs) - m_ref[:, hs])
             dv = dv + mm(p.astype(BF16), gs[hs, :], NN)
             dp = mm(kv[1, r], gs[hs, :], NT)
@@ -420,14 +453,12 @@
         part[r] = jnp.where(half == 0, dv, dk).astype(BF16)
         to_twin(r).start()
 
-        @pl.when(r < SUPS)
+        @pl.when(i > 0)
         def _():
-            rs_send[r + 1] = both_cores(r + 1).astype(BF16)
-            to_owner(r + 1).start()
-
-        @pl.when(r == SUPS)
-        def _():
-            z_fill(0, obf)
+            done = crossing_first(i - 1)
+            rs_send[done] = both_cores(done).astype(BF16)
+            to_owner(done).start()
+
 
     dqbf[...] = (dqt[...] * SCALE).astype(BF16)
     z_fill(1, dqbf)
@@ -437,18 +468,16 @@
         landed(rs_recv.at[r], rs_rs.at[r])
         terms = terms + rs_recv[r].astype(F32)
     rows = (terms * jnp.where(half == 0, SCALE, 1.0)).astype(BF16)
-    zsend_k[...] = mm(azk[...], rows, NN).astype(BF16).reshape(ZN, ZK, HD)
+    last = mm(azk[...], rows, NN) + extra[0] + extra[1]
+    zsend_k[...] = last.astype(BF16).reshape(ZN, ZK, HD)
     z_start(2)
     x_fill(1)
-    finish(0, o_out)
     z_wait(2)
     rows = zrecv_k[...].reshape(ZN * ZK, HD)
-    xsend_k[...] = mm(axk[...], rows, NN).astype(BF16).reshape(XN, 2, 64, HD)
+    xsend_k[...] = mm(axk[...], rows, NN).astype(BF16).reshape(XN, PLANES, 64, HD)
     x_start(2)
-    finish(1, dq_out)
-    x_wait(2)
-    dk_out[...] = mm(bfin[...], xrecv_k[0].reshape(256, HD), NN).astype(BF16)
-    dv_out[...] = mm(bfin[...], xrecv_k[1].reshape(256, HD), NN).astype(BF16)
+    for kind in range(3):
+        x_wait(kind)
 
     @pl.loop(0, TP)
     def _(i):
@@ -476,21 +505,48 @@
             left(*x_move(kind, i))
 
 
+def settle(
+    rows_in, rows_k_in, place_in, code_in,
+    o_out, dq_out, dk_out, dv_out,
+    rows, rows_k, place, code, sems,
+):
+    loads = [
+        pltpu.make_async_copy(src, dst, sems.at[i])
+        for i, (src, dst) in enumerate(
+            ((code_in, code), (place_in, place), (rows_k_in, rows_k), (rows_in, rows))
+        )
+    ]
+    for load in loads:
+        load.start()
+    for load in loads:
+        load.wait()
+    late = rows_k[2].reshape(256, HD)
+    lane = lax.broadcasted_iota(jnp.int32, (BLK, 256), 1) & 7
+    found = lax.broadcasted_iota(jnp.int32, (BLK, 256), 0) == code[...]
+    for kind, out in ((0, o_out), (1, dq_out)):
+        for h in range(REP):
+            pick = jnp.where(found & (lane == kind * REP + h), 1.0, 0.0).astype(BF16)
+            both = mm(place[...], rows[kind, h].reshape(256, HD), NN) + mm(pick, late, NN)
+            out[:, h * HD : (h + 1) * HD] = both.astype(BF16)
+    dk_out[...] = mm(place[...], rows_k[0].reshape(256, HD), NN).astype(BF16)
+    dv_out[...] = mm(place[...], rows_k[1].reshape(256, HD), NN).astype(BF16)
+
+
 def body(queries, keys, values, out_grad, doc_lengths, doc_groups):
     anywhere = pl.BlockSpec(memory_space=pl.ANY)
     vmem = pl.BlockSpec(memory_space=pltpu.VMEM)
     wide = REP * HD
     dma = pltpu.SemaphoreType.DMA
-    return pl.pallas_call(
+    moved = pl.pallas_call(
         kernel,
         out_shape=(
-            jax.ShapeDtypeStruct((BLK, wide), BF16),
-            jax.ShapeDtypeStruct((BLK, wide), BF16),
-            jax.ShapeDtypeStruct((BLK, HD), BF16),
-            jax.ShapeDtypeStruct((BLK, HD), BF16),
+            jax.ShapeDtypeStruct((2, REP, XN, 64, HD), BF16),
+            jax.ShapeDtypeStruct((PLANES, XN, 64, HD), BF16),
+            jax.ShapeDtypeStruct((BLK, 256), BF16),
+            jax.ShapeDtypeStruct((1, 256), jnp.int32),
         ),
         in_specs=[anywhere] * 6,
-        out_specs=(vmem, vmem, vmem, vmem),
+        out_specs=(anywhere, anywhere, vmem, vmem),
         scratch_shapes=[
             pltpu.SMEM((NDOC,), jnp.int32),
             pltpu.SMEM((NDOC,), jnp.int32),
@@ -517,14 +573,14 @@
             pltpu.VMEM((ZN, ZK, HD), BF16),
             pltpu.VMEM((ZN, ZK, HD), BF16),
             pltpu.VMEM((2, XN, REP, 64, HD), BF16),
-            pltpu.VMEM((2, REP, XN, 64, HD), BF16),
-            pltpu.VMEM((XN, 2, 64, HD), BF16),
-            pltpu.VMEM((2, XN, 64, HD), BF16),
+            pltpu.VMEM((XN, PLANES, 64, HD), BF16),
             pltpu.VMEM((ZN * ZR, wide), BF16),
             pltpu.VMEM((XN * 256, ZN * ZR), BF16),
             pltpu.VMEM((ZN * ZK, 2 * BLK), BF16),
-            pltpu.VMEM((XN * 128, ZN * ZK), BF16),
-            pltpu.VMEM((BLK, 256), BF16),
+            pltpu.VMEM((XN * 64 * PLANES, ZN * ZK), BF16),
+            pltpu.VMEM((2, ZN * ZK, wide), BF16),
+            pltpu.VMEM((2, ZN * ZK, HD), F32),
+            pltpu.VMEM((1, wide), jnp.int32),
             pltpu.VMEM((1, wide), jnp.int32),
             pltpu.VMEM((1, ZN * ZR), jnp.int32),
             pltpu.VMEM((1, 2 * BLK), jnp.int32),
@@ -551,6 +607,25 @@
             collective_id=0, has_side_effects=True, vmem_limit_bytes=60 * 1024 * 1024
         ),
     )(doc_lengths, doc_groups, queries, keys, values, out_grad)
+    return pl.pallas_call(
+        settle,
+        out_shape=(
+            jax.ShapeDtypeStruct((BLK, wide), BF16),
+            jax.ShapeDtypeStruct((BLK, wide), BF16),
+            jax.ShapeDtypeStruct((BLK, HD), BF16),
+            jax.ShapeDtypeStruct((BLK, HD), BF16),
+        ),
+        in_specs=[anywhere] * 4,
+        out_specs=(vmem,) * 4,
+        scratch_shapes=[
+            pltpu.VMEM((2, REP, XN, 64, HD), BF16),
+            pltpu.VMEM((PLANES, XN, 64, HD), BF16),
+            pltpu.VMEM((BLK, 256), BF16),
+            pltpu.VMEM((1, 256), jnp.int32),
+            dma((4,)),
+        ],
+        compiler_params=pltpu.CompilerParams(vmem_limit_bytes=60 * 1024 * 1024),
+    )(*moved)
 
 
 def solution(mesh):

time: 92.4 us -> 83.5 us (0.904)
  the two profiles are of different devices: /device:TPU:9 before, /device:TPU:1 now
where the time goes in v4:
time: 83.5 us; the launch traced here: 83.3 us
  Pallas kernels  82.7 us (99%)
    pallas_call x1, Pallas kernels, body(): pl.pallas_call(kernel, out_shape=(jax.ShapeDtypeStruct((2, REP, XN, 64, H...  80.4 us
    pallas_call x1, Pallas kernels, body(): pl.pallas_call(settle, out_shape=(jax.ShapeDtypeStruct((BLK, wide), BF16)...  2.31 us

profile of v4, /device:TPU:1, one launch (start us, length us, event | category | flops | bytes accessed | tf_op | source)
XLA Modules:
  0.0 83.3 jit_solution(13697463688960068723)
XLA Ops:
  0.6 80.4 %shard_map.93 = (bf16[2,4,4,64,128]{4,3,2,1,0:T(8,128)(2,1)}, bf16[3,4,64,128]{3,2,1,0:T(8,128)(2,1)}, bf16[128,256]{1,0:T(8,128)(2,1)}, s32[1,256]{1,0:T(1,128)}) custom-call(s32[8]{0:T(128)} %len_in.1, s32[8]{0:T(128)} %grp_in.1, bf16[16,4096]{1,0:T(8,128)(2,1)} %q_in.1, bf16[16,1024]{1,0:T(8,128)(2,1)} %k_in.1, bf16[16,1024]{1,0:T(8,128)(2,1)} %v_in.1, ...), custom_call_target="tpu_custom_call" | custom-call | tf_op jit(solution)/shard_map/pallas_call | solution.py:540
  81.0 2.3 %shard_map.94 = (bf16[128,512]{1,0:T(8,128)(2,1)}, bf16[128,512]{1,0:T(8,128)(2,1)}, bf16[128,128]{1,0:T(8,128)(2,1)}, bf16[128,128]{1,0:T(8,128)(2,1)}) custom-call(bf16[2,4,4,64,128]{4,3,2,1,0:T(8,128)(2,1)} %get-tuple-element.8.rows_in, bf16[3,4,64,128]{3,2,1,0:T(8,128)(2,1)} %get-tuple-element.9.rows_k_in, bf16[128,256]{1,0:T(8,128)(2,1)} %get-tuple-element.10.place_in, ...), custom_call_target="tpu_custom_call" | custom-call | tf_op jit(solution)/shard_map/pallas_call | solution.py:610

commit v5 on v4

--- a/solution.py
+++ b/solution.py
@@ -163,11 +163,12 @@
         for kind in range(2):
             start_to(*kv_piece(kind, (head + far_first(i, TP)) % TP))
 
-    for kind in range(2):
-
+    def wide_start(kind):
         @pl.loop(0, TP)
-        def _(i, kind=kind):
+        def _(i):
             start_to(*wide_piece(kind, (head + far_first(i, TP)) % TP))
+
+    wide_start(0)
 
     pltpu.make_async_copy(len_in, len_ref, loc_s.at[0]).wait()
     pltpu.make_async_copy(grp_in, grp_ref, loc_s.at[1]).wait()
@@ -302,17 +303,15 @@
         landed(kv.at[half, r], ag_rs.at[r])
         across(r).start()
 
-    def crossing_first(t):
-        return t + 1
-
     def crossing_last(t):
         return jnp.where(t < SUPS // 2, 2 * t + 2, 2 * t + 1 - SUPS)
 
-    @pl.loop(0, SUPS)
-    def _(t):
-        gather(crossing_first(t)).start()
+    @pl.loop(1, SUPS + 1)
+    def _(r):
+        gather(r).start()
 
     across(0).start()
+    wide_start(1)
 
     def wide_landed(kind):
         @pl.loop(0, TP)
@@ -331,7 +330,9 @@
 
     def scores(r, hs):
         raw = mm(kv[0, r], qs[hs, :], NT) * SCALE2
-        place_in = lax.broadcasted_iota(jnp.int32, raw.shape, 0) - 2 * BLK * r
+        place_in = lax.broadcasted_iota(jnp.int32, raw.shape, 0)
+        if not isinstance(r, int):
+            return jnp.where(place_in >= low_ref[:, hs] + 2 * BLK * r, raw, NEG)
         query = (lax.broadcasted_iota(jnp.int32, raw.shape, 1) & (BLK - 1)) + half * BLK
         return jnp.where((place_in <= query) & (place_in >= low_ref[:, hs]), raw, NEG)
 
@@ -406,12 +407,22 @@
     def x_start(kind):
         @pl.loop(0, XN)
         def _(i):
-            start_to(*x_move(kind, (xi + i) % XN))
+            start_to(*x_move(kind, (xi + far_first(i, XN)) % XN))
 
     def x_wait(kind):
         @pl.loop(0, XN)
         def _(i):
             landed(xbuf[kind][1].at[:, i], x_rs.at[kind, i])
+
+    def z_left(kind):
+        @pl.loop(0, ZN)
+        def _(i):
+            left(*z_move(kind, i))
+
+    def x_left(kind):
+        @pl.loop(0, XN)
+        def _(i):
+            left(*x_move(kind, i))
 
     def z_fill(kind, src):
         zsend[kind] = mm(az[...], src[...], NT).astype(BF16).reshape(ZN, ZR, HD)
@@ -437,9 +448,7 @@
     dqt[...] = jnp.zeros_like(dqt)
     z_fill(0, obf)
 
-    @pl.loop(0, SUPS + 1)
-    def _(i):
-        r = jnp.where(i < SUPS, crossing_first(i), 0)
+    def terms_of(r):
         dk = jnp.zeros((2 * BLK, HD), F32)
         dv = jnp.zeros((2 * BLK, HD), F32)
         for hs in pairs:
@@ -453,13 +462,20 @@
         part[r] = jnp.where(half == 0, dv, dk).astype(BF16)
         to_twin(r).start()
 
-        @pl.when(i > 0)
+    def pass_on(r):
+        rs_send[r] = both_cores(r).astype(BF16)
+        to_owner(r).start()
+
+    @pl.loop(1, SUPS + 1)
+    def _(r):
+        terms_of(r)
+
+        @pl.when(r > 1)
         def _():
-            done = crossing_first(i - 1)
-            rs_send[done] = both_cores(done).astype(BF16)
-            to_owner(done).start()
-
-
+            pass_on(r - 1)
+
+    terms_of(0)
+    pass_on(SUPS)
     dqbf[...] = (dqt[...] * SCALE).astype(BF16)
     z_fill(1, dqbf)
     x_fill(0)
@@ -472,12 +488,6 @@
     zsend_k[...] = last.astype(BF16).reshape(ZN, ZK, HD)
     z_start(2)
     x_fill(1)
-    z_wait(2)
-    rows = zrecv_k[...].reshape(ZN * ZK, HD)
-    xsend_k[...] = mm(axk[...], rows, NN).astype(BF16).reshape(XN, PLANES, 64, HD)
-    x_start(2)
-    for kind in range(3):
-        x_wait(kind)
 
     @pl.loop(0, TP)
     def _(i):
@@ -494,15 +504,19 @@
 
     across(0).wait_send()
     to_twin(0).wait_send()
+    z_left(0)
+    z_left(1)
+    x_left(0)
+    z_wait(2)
+    rows = zrecv_k[...].reshape(ZN * ZK, HD)
+    xsend_k[...] = mm(axk[...], rows, NN).astype(BF16).reshape(XN, PLANES, 64, HD)
+    x_start(2)
+    z_left(2)
+    x_left(1)
     for kind in range(3):
-
-        @pl.loop(0, ZN)
-        def _(i, kind=kind):
-            left(*z_move(kind, i))
-
-        @pl.loop(0, XN)
-        def _(i, kind=kind):
-            left(*x_move(kind, i))
+        x_wait(kind)
+
+    x_left(2)
 
 
 def settle(

time: 83.5 us -> 82.4 us (0.987)
  the two profiles are of different devices: /device:TPU:1 before, /device:TPU:9 now
where the time goes in v5:
time: 82.4 us; the launch traced here: 80.8 us
  Pallas kernels  80.2 us (97%)
    pallas_call x1, Pallas kernels, body(): pl.pallas_call(kernel, out_shape=(jax.ShapeDtypeStruct((2, REP, XN, 64, H...  77.8 us
    pallas_call x1, Pallas kernels, body(): pl.pallas_call(settle, out_shape=(jax.ShapeDtypeStruct((BLK, wide), BF16)...  2.31 us

profile of v5, /device:TPU:9, one launch (start us, length us, event | category | flops | bytes accessed | tf_op | source)
XLA Modules:
  0.0 80.8 jit_solution(13076135947676309742)
XLA Ops:
  0.6 77.8 %shard_map.93 = (bf16[2,4,4,64,128]{4,3,2,1,0:T(8,128)(2,1)}, bf16[3,4,64,128]{3,2,1,0:T(8,128)(2,1)}, bf16[128,256]{1,0:T(8,128)(2,1)}, s32[1,256]{1,0:T(1,128)}) custom-call(s32[8]{0:T(128)} %len_in.1, s32[8]{0:T(128)} %grp_in.1, bf16[16,4096]{1,0:T(8,128)(2,1)} %q_in.1, bf16[16,1024]{1,0:T(8,128)(2,1)} %k_in.1, bf16[16,1024]{1,0:T(8,128)(2,1)} %v_in.1, ...), custom_call_target="tpu_custom_call" | custom-call | tf_op jit(solution)/shard_map/pallas_call | solution.py:554
  78.5 2.3 %shard_map.94 = (bf16[128,512]{1,0:T(8,128)(2,1)}, bf16[128,512]{1,0:T(8,128)(2,1)}, bf16[128,128]{1,0:T(8,128)(2,1)}, bf16[128,128]{1,0:T(8,128)(2,1)}) custom-call(bf16[2,4,4,64,128]{4,3,2,1,0:T(8,128)(2,1)} %get-tuple-element.8.rows_in, bf16[3,4,64,128]{3,2,1,0:T(8,128)(2,1)} %get-tuple-element.9.rows_k_in, bf16[128,256]{1,0:T(8,128)(2,1)} %get-tuple-element.10.place_in, ...), custom_call_target="tpu_custom_call" | custom-call | tf_op jit(solution)/shard_map/pallas_call | solution.py:624
